TPU v7x, 32 devices: a whole 2x2x4 slice. The times are simulated.
32 devices in a mesh: cluster: 4 (over x, core), row: 8 (over z, y).
Axes of the slice: x: 2, y: 2, z: 4, core: 2. Of those that a mesh axis runs over, the one named last changes fastest.
Arguments:
- sources: bfloat16 [8192, 512], P(('cluster', 'row')), may hold values from -12 to 12
- targets: bfloat16 [8192, 512], P(('cluster', 'row')), may hold values from -12 to 12
- source_order: int32 [8192], P(('cluster', 'row')), may hold values from 0 to 255, as said below
- target_order: int32 [8192], P(('cluster', 'row')), may hold values from 0 to 255, as said below
Outputs:
- source_map: bfloat16 [8192, 512], P(('cluster', 'row'))
- target_map: bfloat16 [8192, 512], P(('cluster', 'row'))
Inputs may be any that keep to these rules, and one draw needn't show every extreme that they name: `source_order`: in each aligned block of 256 consecutive rows every value appears exactly once, so each block holds 64 source rows of every co-cluster. `target_order`: in each aligned block of 256 consecutive rows every value appears exactly once, so each block holds 64 target rows of every co-cluster.
All inputs are finite; a program needn't handle non-finite values.
Results may differ from a plain program's by a relative error of at most 0.01.
Values may be sent and summed in bfloat16 or wider, within the bound.
A program may use at most 64 MiB of HBM per device.

v0:
```python
import math

import jax
import jax.numpy as jnp
from jax import lax
from jax.sharding import PartitionSpec as P

ITERS = 3


entropy_weight = 0.02


def square_sums(matrix):
    widened = matrix.astype(jnp.float32)
    return jnp.sum(widened * widened, axis=1)


def cost_panel(source_rows, source_norms, target_rows, target_norms):
    inner = jnp.einsum("id,jd->ij", source_rows, target_rows, preferred_element_type=jnp.float32)
    return (source_norms[:, None] + target_norms[None, :] - 2.0 * inner) / source_rows.shape[1]


def into_slots(ordering, matrix):
    positions = jnp.arange(matrix.shape[0], dtype=jnp.int32)
    selector = (positions[:, None] == ordering[None, :]).astype(jnp.bfloat16)
    return jnp.dot(selector, matrix, preferred_element_type=jnp.float32).astype(jnp.bfloat16)


def out_of_slots(ordering, matrix):
    positions = jnp.arange(matrix.shape[0], dtype=jnp.int32)
    selector = (ordering[:, None] == positions[None, :]).astype(jnp.bfloat16)
    return jnp.dot(selector, matrix, preferred_element_type=jnp.float32).astype(jnp.bfloat16)


def shards(sources, targets, source_order, target_order):
    rows_dev = sources.shape[0]
    width = sources.shape[1]
    sent_sources = into_slots(source_order, sources)
    sent_targets = into_slots(target_order, targets)
    local_sources, local_targets = (
        lax.all_to_all(sent_sources, "cluster", split_axis=0, concat_axis=0, tiled=True),
        lax.all_to_all(sent_targets, "cluster", split_axis=0, concat_axis=0, tiled=True),
    )
    cluster_targets = lax.all_gather(local_targets, "row", axis=0, tiled=True)
    columns = cluster_targets.shape[0]
    span = 512
    pieces = columns // span
    target_norms = square_sums(cluster_targets)
    target_blocks = cluster_targets.reshape(pieces, span, width)
    norm_blocks = target_norms.reshape(pieces, span)
    source_norms = square_sums(local_sources)
    log_mass = -math.log(columns)

    def row_lse(potential):

        def row_advance(carry, item):
            running, totals = carry
            block, block_norms, block_potential = item
            scores = (
                block_potential[None, :]
                - cost_panel(local_sources, source_norms, block, block_norms)
            ) / entropy_weight
            highest = jnp.maximum(running, jnp.max(scores, axis=1))
            totals = totals * jnp.exp(running - highest) + jnp.sum(
                jnp.exp(scores - highest[:, None]), axis=1
            )
            return ((highest, totals), None)

        start = (jnp.full((rows_dev,), -jnp.inf, jnp.float32), jnp.zeros((rows_dev,), jnp.float32))
        (running, totals), unused = lax.scan(
            row_advance, start, (target_blocks, norm_blocks, potential.reshape(pieces, span))
        )
        return running + jnp.log(totals)

    def column_lse(source_potential):

        def column_advance(carry, item):
            block, block_norms = item
            scores = (
                source_potential[:, None]
                - cost_panel(local_sources, source_norms, block, block_norms)
            ) / entropy_weight
            highest = jnp.max(scores, axis=0)
            return (carry, (highest, jnp.sum(jnp.exp(scores - highest[None, :]), axis=0)))

        unused, (peaks, totals) = lax.scan(column_advance, 0, (target_blocks, norm_blocks))
        peaks = peaks.reshape(-1)
        totals = totals.reshape(-1)
        highest = lax.pmax(peaks, "row")
        summed = lax.psum(totals * jnp.exp(peaks - highest), "row")
        return highest + jnp.log(summed)

    target_potential = jnp.zeros((columns,), jnp.float32)
    for repeat in range(ITERS):
        source_potential = entropy_weight * (log_mass - row_lse(target_potential))
        column_norm = column_lse(source_potential)
        target_potential = entropy_weight * (log_mass - column_norm)
    every_potential = lax.all_gather(source_potential, "row", axis=0, tiled=True)
    own_start = lax.axis_index("row") * rows_dev
    own_norm = lax.dynamic_slice_in_dim(column_norm, own_start, rows_dev, 0)
    own_target_norms = square_sums(local_targets)
    piece = lax.all_gather(local_sources, "row", axis=0, tiled=True)
    scores = (
        every_potential[:, None]
        - cost_panel(piece, square_sums(piece), local_targets, own_target_norms)
    ) / entropy_weight
    weights = jnp.exp(scores - own_norm[None, :]).astype(jnp.bfloat16)
    target_map = jnp.einsum("ij,id->jd", weights, piece, preferred_element_type=jnp.float32).astype(
        jnp.bfloat16
    )
    row_norm = row_lse(target_potential)

    def accumulate(carry, item):
        block, block_norms, block_potential = item
        scores = (
            block_potential[None, :] - cost_panel(local_sources, source_norms, block, block_norms)
        ) / entropy_weight
        weights = jnp.exp(scores - row_norm[:, None]).astype(jnp.bfloat16)
        return (carry + jnp.dot(weights, block, preferred_element_type=jnp.float32), None)

    source_sums, unused = lax.scan(
        accumulate,
        jnp.zeros((rows_dev, width), jnp.float32),
        (target_blocks, norm_blocks, target_potential.reshape(pieces, span)),
    )
    source_map = source_sums.astype(jnp.bfloat16)
    back_sources, back_targets = (
        lax.all_to_all(source_map, "cluster", split_axis=0, concat_axis=0, tiled=True),
        lax.all_to_all(target_map, "cluster", split_axis=0, concat_axis=0, tiled=True),
    )
    return (out_of_slots(source_order, back_sources), out_of_slots(target_order, back_targets))


def solution(mesh):
    return jax.shard_map(
        shards,
        mesh=mesh,
        in_specs=(
            P(("cluster", "row"), None),
            P(("cluster", "row"), None),
            P(("cluster", "row")),
            P(("cluster", "row")),
        ),
        out_specs=(P(("cluster", "row"), None), P(("cluster", "row"), None)),
        check_vma=False,
    )
```

profile of v0, /device:TPU:0, one launch (start us, length us, event | category | flops | bytes accessed | tf_op | source)
XLA Modules:
  0.0 281.4 jit_solution(16834470115758187477)
XLA Ops:
  7.2 0.9 copy-done
  8.1 0.9 convolution_convert_fusion.3
  9.0 10.2 %all_to_all.48 = bf16[4,64,512]{2,1,0:T(8,128)(2,1)} all-to-all(bf16[4,64,512]{2,1,0:T(8,128)(2,1)S(1)} %bitcast.262), channel_id=1, replica_groups=mesh['cluster'=4,'row'=8] {'cluster'}, dimensions={0} | all-to-all | bytes 524288 | tf_op jit(solution)/shard_map/all_to_all | solution.py:43
  19.2 1.9 convolution_convert_fusion.4
  21.1 3.4 %all-to-all-start = ((bf16[4,64,512]{2,1,0:T(8,128)(2,1)}), bf16[4,64,512]{2,1,0:T(8,128)(2,1)S(1)}, u32[]{:S(2)}, u32[]{:S(2)}) async-start(bf16[4,64,512]{2,1,0:T(8,128)(2,1)} %bitcast.15), calls=%async_computation | async-start | bytes 524288 | tf_op jit(solution)/shard_map/all_to_all | solution.py:42
  24.7 5.9 %all-to-all-done = bf16[4,64,512]{2,1,0:T(8,128)(2,1)S(1)} async-done(((bf16[4,64,512]{2,1,0:T(8,128)(2,1)}), bf16[4,64,512]{2,1,0:T(8,128)(2,1)S(1)}, u32[]{:S(2)}, u32[]{:S(2)}) %all-to-all-start) | async-done | bytes 262176 | tf_op jit(solution)/shard_map/all_to_all | solution.py:42
  30.8 1.1 multiply_reduce_fusion.2
  32.0 37.4 %all-gather.4.cloned.1.call-done = bf16[2048,512]{1,0:T(8,128)(2,1)} async-done(((bf16[256,512]{1,0:T(8,128)(2,1)}), bf16[2048,512]{1,0:T(8,128)(2,1)}) %all-gather.4.cloned.1.call-update) | async-done | bytes 2097168 | tf_op jit(solution)/shard_map/all_gather | solution.py:45
  69.4 2.1 multiply_reduce_fusion.1
  71.5 6.4 %while.102 = (s32[]{:T(128)}, f32[256]{0:T(256)S(1)}, f32[256]{0:T(256)S(1)}, f32[256]{0:T(256)S(1)}, f32[4,512]{1,0:T(4,128)S(1)}, /*index=5*/bf16[4,512,512]{2...) while((s32[]{:T(128)}, f32[256]{0:T(256)S(1)}, f32[256]{0:T(256)S(1)}, ...), condition=%wide.region_5.6_spmd.clone, body=%wide.region_2.5_spmd.clone.sunk | while | flops 135398656 | bytes 1855608 | solution.py:71
  71.5 1.4 fusion.157
  73.1 1.4 fusion.157
  74.7 1.4 fusion.157
  76.3 1.4 fusion.157
  77.9 6.8 %while.99 = (s32[]{:T(128)}, f32[4,512]{1,0:T(4,128)S(1)}, f32[4,512]{1,0:T(4,128)S(1)}, f32[256]{0:T(256)S(1)}, f32[256]{0:T(256)S(1)}, /*index=5*/f32[4,512]{1...) while((s32[]{:T(128)}, f32[4,512]{1,0:T(4,128)S(1)}, ...), condition=%wide.region_9.10_spmd, body=%wide.region_6.9_spmd.sunk | while | flops 135396352 | bytes 1857661 | solution.py:87
  77.9 1.5 fusion.151
  79.6 1.4 fusion.151
  81.3 1.4 fusion.151
  83.0 1.4 fusion.151
  84.7 19.3 %pmax.21 = f32[2048]{0:T(1024)S(1)} all-reduce(f32[2048]{0:T(1024)S(1)} %bitcast.269), channel_id=1, replica_groups=mesh['cluster'=4,'row'=8] {'row'}, use_global_device_ids=true, to_apply=%region_10.11 | all-reduce | flops 2048 | bytes 16384 | tf_op jit(solution)/shard_map/pmax | solution.py:90
  104.0 18.0 %psum.21 = f32[2048]{0:T(1024)S(1)} all-reduce(f32[2048]{0:T(1024)S(1)} %exponential_multiply_fusion.2), channel_id=1, replica_groups=mesh['cluster'=4,'row'=8] {'row'}, use_global_device_ids=true, to_apply=%region_11.12 | all-reduce | flops 2048 | bytes 16384 | tf_op jit(solution)/shard_map/psum | solution.py:91
  122.1 6.4 %while.103 = (s32[]{:T(128)}, f32[256]{0:T(256)S(1)}, f32[256]{0:T(256)S(1)}, f32[4,512]{1,0:T(4,128)S(1)}, f32[256]{0:T(256)S(1)}, /*index=5*/f32[4,512]{1,0:T(...) while((s32[]{:T(128)}, f32[256]{0:T(256)S(1)}, ...), condition=%wide.region_15.16_spmd.clone, body=%wide.region_12.15_spmd.clone.sunk | while | flops 135398656 | bytes 1861760 | solution.py:71
  122.1 1.4 fusion.161
  123.7 1.4 fusion.161
  125.3 1.4 fusion.161
  126.9 1.4 fusion.161
  128.5 6.7 %while.100 = (s32[]{:T(128)}, f32[4,512]{1,0:T(4,128)S(1)}, f32[4,512]{1,0:T(4,128)S(1)}, f32[256]{0:T(256)S(1)}, f32[256]{0:T(256)S(1)}, /*index=5*/f32[4,512]{...) while((s32[]{:T(128)}, f32[4,512]{1,0:T(4,128)S(1)}, ...), condition=%wide.region_19.20_spmd, body=%wide.region_16.19_spmd.sunk | while | flops 135396352 | bytes 1857661 | solution.py:87
  128.5 1.4 fusion.153
  130.2 1.4 fusion.153
  131.9 1.4 fusion.153
  133.6 1.4 fusion.153
  135.3 19.2 %pmax.22 = f32[2048]{0:T(1024)S(1)} all-reduce(f32[2048]{0:T(1024)S(1)} %bitcast.271), channel_id=1, replica_groups=mesh['cluster'=4,'row'=8] {'row'}, use_global_device_ids=true, to_apply=%region_20.21 | all-reduce | flops 2048 | bytes 16384 | tf_op jit(solution)/shard_map/pmax | solution.py:90
  154.5 17.5 %psum.22 = f32[2048]{0:T(1024)S(1)} all-reduce(f32[2048]{0:T(1024)S(1)} %exponential_multiply_fusion.1), channel_id=1, replica_groups=mesh['cluster'=4,'row'=8] {'row'}, use_global_device_ids=true, to_apply=%region_21.22 | all-reduce | flops 2048 | bytes 16384 | tf_op jit(solution)/shard_map/psum | solution.py:91
  172.1 6.4 %while.104 = (s32[]{:T(128)}, f32[256]{0:T(256)S(1)}, f32[256]{0:T(256)S(1)}, f32[4,512]{1,0:T(4,128)S(1)}, f32[256]{0:T(256)S(1)}, /*index=5*/f32[4,512]{1,0:T(...) while((s32[]{:T(128)}, f32[256]{0:T(256)S(1)}, ...), condition=%wide.region_25.26_spmd.clone, body=%wide.region_22.25_spmd.clone.sunk | while | flops 135398656 | bytes 1861760 | solution.py:71
  172.1 1.4 fusion.165
  173.7 1.4 fusion.165
  175.3 1.4 fusion.165
  176.9 1.4 fusion.165
  178.6 6.7 %while.101 = (s32[]{:T(128)}, f32[4,512]{1,0:T(4,128)S(1)}, f32[4,512]{1,0:T(4,128)S(1)}, f32[256]{0:T(256)S(1)}, f32[256]{0:T(256)S(1)}, /*index=5*/f32[4,512]{...) while((s32[]{:T(128)}, f32[4,512]{1,0:T(4,128)S(1)}, ...), condition=%wide.region_29.30_spmd, body=%wide.region_26.29_spmd.sunk | while | flops 135396352 | bytes 1857661 | solution.py:87
  178.6 1.4 fusion.155
  180.3 1.4 fusion.155
  182.0 1.4 fusion.155
  183.6 1.4 fusion.155
  185.3 19.3 %pmax.23 = f32[2048]{0:T(1024)S(1)} all-reduce(f32[2048]{0:T(1024)S(1)} %bitcast.273), channel_id=1, replica_groups=mesh['cluster'=4,'row'=8] {'row'}, use_global_device_ids=true, to_apply=%region_30.31 | all-reduce | flops 2048 | bytes 16384 | tf_op jit(solution)/shard_map/pmax | solution.py:90
  204.7 17.5 %psum.23 = f32[2048]{0:T(1024)S(1)} all-reduce(f32[2048]{0:T(1024)S(1)} %exponential_multiply_fusion), channel_id=1, replica_groups=mesh['cluster'=4,'row'=8] {'row'}, use_global_device_ids=true, to_apply=%region_31.32 | all-reduce | flops 2048 | bytes 16384 | tf_op jit(solution)/shard_map/psum | solution.py:91
  222.2 6.4 %while.105 = (s32[]{:T(128)}, f32[256]{0:T(256)S(1)}, f32[256]{0:T(256)S(1)}, f32[4,512]{1,0:T(4,128)S(1)}, f32[256]{0:T(256)S(1)}, /*index=5*/f32[4,512]{1,0:T(...) while((s32[]{:T(128)}, f32[256]{0:T(256)S(1)}, ...), condition=%wide.region_35.36_spmd.clone, body=%wide.region_32.35_spmd.clone.sunk | while | flops 135398656 | bytes 1861760 | solution.py:71
  222.2 1.4 fusion.169
  223.8 1.4 fusion.169
  225.4 1.4 fusion.169
  227.0 1.4 fusion.169
  228.6 7.7 %while.106 = (s32[]{:T(128)}, f32[256,512]{1,0:T(8,128)S(1)}, f32[4,512]{1,0:T(4,128)S(1)}, f32[256]{0:T(256)S(1)}, f32[4,512]{1,0:T(4,128)S(1)}, /*index=5*/bf1...) while((s32[]{:T(128)}, f32[256,512]{1,0:T(8,128)S(1)}, ...), condition=%wide.region_37.38_spmd.clone, body=%wide.region_36.37_spmd.clone.sunk | while | flops 269746176 | bytes 2375290 | solution.py:122
  228.7 1.9 convolution_add_fusion.2
  230.6 1.9 convolution_add_fusion.2
  232.5 1.9 convolution_add_fusion.2
  234.4 1.9 convolution_add_fusion.2
  236.3 0.7 convert_element_type.46
  237.1 3.4 %all-to-all-start.2 = ((bf16[4,64,512]{2,1,0:T(8,128)(2,1)}), bf16[4,64,512]{2,1,0:T(8,128)(2,1)S(1)}, u32[]{:S(2)}, u32[]{:S(2)}) async-start(bf16[4,64,512]{2,1,0:T(8,128)(2,1)} %bitcast.20), calls=%async_computation.2 | async-start | bytes 524288 | tf_op jit(solution)/shard_map/all_to_all | solution.py:129
  240.6 18.2 %all-gather = f32[8,1,256]{2,1,0:T(1,128)S(1)} all-gather(f32[1,1,256]{2,1,0:T(1,128)S(1)} %bitcast.297), channel_id=1, replica_groups=mesh['cluster'=4,'row'=8] {'row'}, dimensions={0}, use_global_device_ids=true | all-gather | bytes 9216 | tf_op jit(solution)/shard_map/all_gather | solution.py:99
  258.8 2.2 multiply_reduce_fusion
  261.1 3.1 %convolution_convert_fusion.1 = bf16[256,512]{1,0:T(8,128)(2,1)} fusion(bf16[2048,512]{1,0:T(8,128)(2,1)S(1)} %copy-done.4, bf16[256,512]{1,0:T(8,128)(2,1)S(1)} %bitcast.256, f32[256]{0:T(256)S(1)} %dynamic_slice.66, f32[256]{0:T(256)S(1)} %add.212, f32[2048]{0:T(1024)S(1)} %multiply_reduce_fusion, f32[2048]{0:T(1024)S(1)} %bitcast.296), kind=kOutput, calls=%fused_computation.133 | convolution fusion | flops 1078067200 | bytes 2639872 | tf_op jit(solution)/shard_map/ij,id->jd/dot_general | solution.py:109
  264.2 3.4 %all-to-all-start.3 = ((bf16[4,64,512]{2,1,0:T(8,128)(2,1)}), bf16[4,64,512]{2,1,0:T(8,128)(2,1)S(1)}, u32[]{:S(2)}, u32[]{:S(2)}) async-start(bf16[4,64,512]{2,1,0:T(8,128)(2,1)} %bitcast.24), calls=%async_computation.3 | async-start | bytes 524288 | tf_op jit(solution)/shard_map/all_to_all | solution.py:130
  267.6 1.0 convolution_convert_fusion.2
  268.6 5.0 %all-to-all-done.3 = bf16[4,64,512]{2,1,0:T(8,128)(2,1)S(1)} async-done(((bf16[4,64,512]{2,1,0:T(8,128)(2,1)}), bf16[4,64,512]{2,1,0:T(8,128)(2,1)S(1)}, u32[]{:S(2)}, u32[]{:S(2)}) %all-to-all-start.3) | async-done | bytes 262176 | tf_op jit(solution)/shard_map/all_to_all | solution.py:130
  273.6 1.0 convolution_convert_fusion
  (190 shorter events, 5.8 us)
Async XLA Ops:
  7.2 1.0 copy-start
  7.2 62.2 %all-gather.4.cloned.1.call-start = ((), (), s32[]{:S(2)}) async-start(), calls=%async_computation.4 | async-start | bytes 2359296 | tf_op jit(solution)/shard_map/all_gather | solution.py:45
  21.1 9.4 %all-to-all-start = ((bf16[4,64,512]{2,1,0:T(8,128)(2,1)}), bf16[4,64,512]{2,1,0:T(8,128)(2,1)S(1)}, u32[]{:S(2)}, u32[]{:S(2)}) async-start(bf16[4,64,512]{2,1,0:T(8,128)(2,1)} %bitcast.15), calls=%async_computation | async-start | bytes 524288 | tf_op jit(solution)/shard_map/all_to_all | solution.py:42
  24.5 234.2 %all-gather.6.cloned.1.call-start = ((), (), s32[]{:S(2)}) async-start(), calls=%async_computation.5 | async-start | bytes 2359296 | tf_op jit(solution)/shard_map/all_gather | solution.py:103
  30.5 1.4 copy-start.2
  32.0 39.5 %copy-start.3 = (bf16[4,64,512]{2,1,0:T(8,128)(2,1)S(1)}, bf16[4,64,512]{2,1,0:T(8,128)(2,1)}, u32[]{:S(2)}) copy-start(bf16[4,64,512]{2,1,0:T(8,128)(2,1)} %copy-done.2) | copy-start | bytes 786436
  236.3 24.7 %copy-start.1 = (bf16[4,64,512]{2,1,0:T(8,128)(2,1)S(1)}, bf16[4,64,512]{2,1,0:T(8,128)(2,1)}, u32[]{:S(2)}) copy-start(bf16[4,64,512]{2,1,0:T(8,128)(2,1)} %all_to_all.48) | copy-start | bytes 786436
  237.1 27.1 %all-to-all-start.2 = ((bf16[4,64,512]{2,1,0:T(8,128)(2,1)}), bf16[4,64,512]{2,1,0:T(8,128)(2,1)S(1)}, u32[]{:S(2)}, u32[]{:S(2)}) async-start(bf16[4,64,512]{2,1,0:T(8,128)(2,1)} %bitcast.20), calls=%async_computation.2 | async-start | bytes 524288 | tf_op jit(solution)/shard_map/all_to_all | solution.py:129
  258.8 2.2 copy-start.4
  261.0 6.6 %copy-start.5 = (s32[256]{0:T(256)S(1)}, s32[256]{0:T(256)}, u32[]{:S(2)}) copy-start(s32[256]{0:T(256)} %param.22) | copy-start | bytes 3076
  261.0 12.6 %copy-start.6 = (s32[256]{0:T(256)S(1)}, s32[256]{0:T(256)}, u32[]{:S(2)}) copy-start(s32[256]{0:T(256)} %param.23) | copy-start | bytes 3076
  264.2 9.4 %all-to-all-start.3 = ((bf16[4,64,512]{2,1,0:T(8,128)(2,1)}), bf16[4,64,512]{2,1,0:T(8,128)(2,1)S(1)}, u32[]{:S(2)}, u32[]{:S(2)}) async-start(bf16[4,64,512]{2,1,0:T(8,128)(2,1)} %bitcast.24), calls=%async_computation.3 | async-start | bytes 524288 | tf_op jit(solution)/shard_map/all_to_all | solution.py:130
Sparse Core Ops, SparseCore 0:
  19.3 50.0 all-gather.3
  72.1 48.8 all-gather.5
where the time goes:
time: 283 us; the launch traced here: 281 us
  blocking collectives  139 us (49%)
  matrix products  55.1 us (19%)
  waiting for transfers between devices  48.3 us (17%)
  between operations  14.5 us (5%)
  starting transfers between devices  10.3 us (4%)
  other arithmetic  10 us (4%)
    pmax x3, blocking collectives, column_lse(): highest = lax.pmax(peaks, 'row')  57.9 us
    psum x3, blocking collectives, column_lse(): summed = lax.psum(totals * jnp.exp(peaks - highest), 'row')  53.1 us
    dot_general x28, matrix products, cost_panel(): jnp.einsum('id,jd->ij', source_rows, target_rows, preferred_element_type=...  39.7 us
    all_gather x1, waiting for transfers between devices, shards(): cluster_targets = lax.all_gather(local_targets, 'row', axis=0, tiled=True)  37.4 us
    all_gather x1, blocking collectives, shards(): lax.all_gather(source_potential, 'row', axis=0, tiled=True)  18.2 us
    all_to_all x1, blocking collectives, shards(): lax.all_to_all(sent_targets, 'cluster', split_axis=0, concat_axis=0, tile...  10.2 us
    dot_general x4, matrix products, accumulate(): jnp.dot(weights, block, preferred_element_type=jnp.float32)  7.51 us
    all_to_all x1, waiting for transfers between devices, shards(): lax.all_to_all(sent_sources, 'cluster', split_axis=0, concat_axis=0, tile...  5.86 us
  transfers between devices with their start and end apart: 5, of which 3 were waited for; matrix products, arithmetic and copies ran while one was open for 23% of the time, Pallas kernels for 0%

commit v1 on v0

v1 whole, which is shorter than its diff:
```python
import functools
import math

import jax
import jax.numpy as jnp
from jax import lax
from jax.experimental import pallas as pl
from jax.experimental.pallas import tpu as pltpu
from jax.sharding import PartitionSpec as P

ITERS = 3
entropy_weight = 0.02
LANES = 128
CORES = 2
MESH = pl.DeviceIdType.MESH


def kernel(
    nc, nr, sources, targets, source_order, target_order, source_out, target_out,
    all_s, all_t, sent, maps, back, cost_s, cost_t, potential, source_row, peaks, sums, parts,
    out_send, out_recv, own_send, own_recv, gather_send, gather_recv, part_send, part_recv,
):
    rows, width = sources.shape
    per = rows // nc
    q = nr // nc
    nx = nc // CORES
    columns = all_s.shape[0]
    blocks = columns // LANES
    own_blocks = rows // LANES
    chunks = min(nc, 4)
    group = nc // chunks
    span = rows // chunks
    log_mass = -math.log2(columns)
    scale = math.log2(math.e) / (width * entropy_weight)

    c = lax.axis_index("cluster")
    r = lax.axis_index("row")
    x, core = c // CORES, c % CORES
    k, y = r // q, r % q
    alls = (all_t, all_s)

    def member(mx, mcore, my):
        return (mx * CORES + mcore) * q + my

    def device(mx, mcore, my):
        return (mx * CORES + mcore, k * q + my)

    me = member(x, core, y)

    def line(d):
        return lax.rem(k + d, nc)

    barrier = pltpu.get_barrier_semaphore()
    for d in range(1, nc):
        pl.semaphore_signal(barrier, inc=1, device_id=(c, line(d) * q + y), device_id_type=MESH)
    others = []
    for dx in range(nx):
        for dcore in range(CORES):
            for dy in range(q):
                if dx or dcore or dy:
                    others.append((lax.rem(x + dx, nx), lax.rem(core + dcore, CORES), lax.rem(y + dy, q)))
    for other in others:
        pl.semaphore_signal(barrier, inc=1, device_id=device(*other), device_id_type=MESH)

    def selector(ordering):
        positions = lax.broadcasted_iota(jnp.int32, (rows, rows), 0)
        return (positions == ordering[...]).astype(jnp.float32).astype(jnp.bfloat16)

    def own_rows(t, block, size):
        return alls[t].at[pl.ds(pl.multiple_of(me * rows + block * size, size), size)]

    def into_slots(t, ordering, matrix):
        slots = jnp.dot(selector(ordering), matrix[...], preferred_element_type=jnp.float32)
        sent[t] = slots.astype(jnp.bfloat16)
        own_rows(t, k, per)[...] = sent[t, pl.ds(pl.multiple_of(k * per, per), per)]

    def line_copy(t, d):
        return pltpu.make_async_remote_copy(
            src_ref=sent.at[t, pl.ds(pl.multiple_of(line(d) * per, per), per)],
            dst_ref=own_rows(t, k, per),
            send_sem=own_send.at[t, d],
            recv_sem=own_recv.at[t, d],
            device_id=(c, line(d) * q + y),
            device_id_type=MESH,
        )

    into_slots(0, target_order, targets)
    pl.semaphore_wait(barrier, nc - 1 + nr - 1)
    line_copies = []
    for t in range(2):
        if t == 1:
            into_slots(1, source_order, sources)
        for d in range(1, nc):
            copy = line_copy(t, d)
            copy.start()
            line_copies.append(copy)

    sent_copies = []
    counts = [0, 0]

    def chunk_rows(t, i, owner):
        start = owner * rows + lax.rem(k // group + i, chunks) * span
        return alls[t].at[pl.ds(pl.multiple_of(start, span), span)]

    def forward(t, i, owner, target):
        number = counts[t]
        counts[t] += 1
        owner = member(*owner)
        where = chunk_rows(t, i, owner)
        copy = pltpu.make_async_remote_copy(
            src_ref=where, dst_ref=where,
            send_sem=gather_send.at[t, number], recv_sem=gather_recv.at[t, i, owner],
            device_id=device(*target), device_id_type=MESH,
        )
        copy.start()
        sent_copies.append(copy)

    def arrive(t, i, owner):
        owner = member(*owner)
        where = chunk_rows(t, i, owner)
        pltpu.make_async_remote_copy(
            src_ref=where, dst_ref=where,
            send_sem=gather_send.at[t, 0], recv_sem=gather_recv.at[t, i, owner],
            device_id=device(*others[0]), device_id_type=MESH,
        ).wait_recv()

    def along(i, first, second):
        return (first, second) if i % 2 == 0 else (second, first)

    def at(step, on=None):
        return (lax.rem(x + step[0], nx), core if on is None else on, lax.rem(y + step[1], q))

    def axes(i):
        return (nx, q) if i % 2 == 0 else (q, nx)

    here = (x, core, y)
    sibling_core = CORES - 1 - core
    sibling = (x, sibling_core, y)

    def gather_own(t):
        if group > 1:
            for d in range(1, nc):
                line_copy(t, d).wait_recv()
        for i in range(chunks):
            if group == 1 and i > 0:
                d = nc - i
                pltpu.make_async_remote_copy(
                    src_ref=sent.at[t, pl.ds(0, per)], dst_ref=own_rows(t, line(i), per),
                    send_sem=own_send.at[t, d], recv_sem=own_recv.at[t, d],
                    device_id=(c, line(i) * q + y), device_id_type=MESH,
                ).wait_recv()
            first, second = axes(i)
            for step in range(1, first):
                forward(t, i, here, at(along(i, step, 0)))
            for step in range(1, second):
                forward(t, i, here, at(along(i, 0, step)))
            forward(t, i, here, sibling)

    def gather_first(t):
        for i in range(chunks):
            first, second = axes(i)
            for step in range(1, first):
                owner = at(along(i, step, 0))
                arrive(t, i, owner)
                for turn in range(1, second):
                    forward(t, i, owner, at(along(i, 0, turn)))
                forward(t, i, owner, sibling)

    def gather_second(t):
        for i in range(chunks):
            first, second = axes(i)
            for step in range(first):
                for turn in range(1, second):
                    owner = at(along(i, step, turn))
                    arrive(t, i, owner)
                    forward(t, i, owner, sibling)

    def gather_sibling(t, owner):
        for i in range(chunks):
            arrive(t, i, owner)

    diagonal = lax.broadcasted_iota(jnp.int32, (LANES, LANES), 0) == lax.broadcasted_iota(
        jnp.int32, (LANES, LANES), 1
    )

    def to_row(column):
        spread = jnp.broadcast_to(column, (LANES, LANES))
        return jnp.sum(jnp.where(diagonal, spread, 0.0), axis=0, keepdims=True)

    def to_column(row):
        spread = jnp.broadcast_to(row, (LANES, LANES))
        return jnp.sum(jnp.where(diagonal, spread, 0.0), axis=1, keepdims=True)

    def square_sums(matrix):
        widened = matrix.astype(jnp.float32)
        return jnp.sum(widened * widened, axis=1, keepdims=True)

    def shard(ref, owner):
        return ref[pl.ds(pl.multiple_of(owner * rows, rows), rows)]

    def build(out, own_ref, all_ref, owners):
        own = shard(own_ref, me)
        own_norms = square_sums(own)

        def panel(index, _):
            owner = owners(index)
            other = shard(all_ref, owner)
            inner = lax.dot_general(
                own, other, (((1,), (1,)), ((), ())), preferred_element_type=jnp.float32
            )
            norms = square_sums(other)
            norms = jnp.concatenate(
                [to_row(norms[b * LANES : (b + 1) * LANES]) for b in range(own_blocks)], axis=1
            )
            out[:, pl.ds(pl.multiple_of(owner * rows, rows), rows)] = scale * (
                2.0 * inner - own_norms - norms
            )
            return 0

        return panel

    def row_lse(cost, row):
        norms = []
        for h in range(own_blocks):
            part = pl.ds(h * LANES, LANES)
            peak = None
            for b in range(blocks):
                scores = cost[part, b * LANES : (b + 1) * LANES] + row[b : b + 1, :]
                peak = scores if peak is None else jnp.maximum(peak, scores)
            peak = jnp.max(peak, axis=1, keepdims=True)
            total = jnp.zeros((LANES, LANES), jnp.float32)
            for b in range(blocks):
                scores = cost[part, b * LANES : (b + 1) * LANES] + row[b : b + 1, :]
                total = total + jnp.exp2(scores - peak)
            norms.append(peak + jnp.log2(jnp.sum(total, axis=1, keepdims=True)))
        return norms

    def column_lse(cost, column):
        for b in range(blocks):
            scores = cost[:, b * LANES : (b + 1) * LANES] + column
            peak = jnp.max(scores, axis=0, keepdims=True)
            peaks[b : b + 1, :] = peak
            sums[b : b + 1, :] = jnp.sum(jnp.exp2(scores - peak), axis=0, keepdims=True)
        return peaks[...] + jnp.log2(sums[...])

    def mapped(cost, row, norms, all_ref):
        norms = jnp.concatenate(norms, axis=0)
        total = jnp.zeros((rows, width), jnp.float32)
        step = 4 * LANES
        for start in range(0, columns, step):
            pieces = []
            for b in range(start // LANES, (start + step) // LANES):
                scores = cost[:, b * LANES : (b + 1) * LANES] + row[b : b + 1, :]
                pieces.append(jnp.exp2(scores - norms).astype(jnp.bfloat16))
            total = total + jnp.dot(
                jnp.concatenate(pieces, axis=1),
                all_ref[start : start + step, :],
                preferred_element_type=jnp.float32,
            )
        return total.astype(jnp.bfloat16)

    gather_own(0)
    gather_first(0)
    gather_second(0)
    gather_own(1)
    panel = build(cost_s, all_s, all_t, lambda index: member(
        index // q, core, lax.rem(index, q)))
    lax.fori_loop(0, nx * q, panel, 0)
    for dx in range(nx):
        for dy in range(q):
            gather_sibling(0, at((dx, dy), sibling_core))
    panel = build(cost_s, all_s, all_t, lambda index: member(
        index // q, sibling_core, lax.rem(index, q)))
    lax.fori_loop(0, nx * q, panel, 0)

    potential[...] = jnp.zeros_like(potential)
    part_copies = []
    for repeat in range(ITERS):
        last = repeat == ITERS - 1
        source_potential = [log_mass - norm for norm in row_lse(cost_s, potential)]
        mine = column_lse(cost_s, jnp.concatenate(source_potential, axis=0))
        parts[repeat, me, 0:blocks, :] = mine
        used = blocks
        if last:
            for b in range(own_blocks):
                parts[repeat, me, blocks + b : blocks + b + 1, :] = to_row(source_potential[b])
            used = blocks + own_blocks
        for number, other in enumerate(others):
            copy = pltpu.make_async_remote_copy(
                src_ref=parts.at[repeat, me, pl.ds(0, used)],
                dst_ref=parts.at[repeat, me, pl.ds(0, used)],
                send_sem=part_send.at[repeat, number],
                recv_sem=part_recv.at[repeat, me],
                device_id=device(*other),
                device_id_type=MESH,
            )
            copy.start()
            part_copies.append(copy)
        if repeat == 0:
            gather_first(1)
        if repeat == 1:
            gather_second(1)
        if last:
            for dx in range(nx):
                for dy in range(q):
                    gather_sibling(1, at((dx, dy), sibling_core))
            lax.fori_loop(0, nr, build(cost_t, all_t, all_s, lambda index: index), 0)
        for number, other in enumerate(others):
            owner = member(*other)
            pltpu.make_async_remote_copy(
                src_ref=parts.at[repeat, owner, pl.ds(0, used)],
                dst_ref=parts.at[repeat, owner, pl.ds(0, used)],
                send_sem=part_send.at[repeat, number],
                recv_sem=part_recv.at[repeat, owner],
                device_id=device(*other),
                device_id_type=MESH,
            ).wait_recv()
        each = [parts[repeat, m, 0:blocks, :] for m in range(nr)]
        peak = functools.reduce(jnp.maximum, each)
        column_norm = peak + jnp.log2(sum(jnp.exp2(one - peak) for one in each))
        potential[...] = log_mass - column_norm
        if last:
            sums[...] = column_norm

    def back_copy(t, d):
        return pltpu.make_async_remote_copy(
            src_ref=maps.at[t, pl.ds(pl.multiple_of(line(d) * per, per), per)],
            dst_ref=back.at[t, pl.ds(pl.multiple_of(k * per, per), per)],
            send_sem=out_send.at[t, d],
            recv_sem=out_recv.at[t, d],
            device_id=(c, line(d) * q + y),
            device_id_type=MESH,
        )

    def send_back(t):
        for d in range(1, nc):
            back_copy(t, d).start()
        own = pl.ds(pl.multiple_of(k * per, per), per)
        back[t, own] = maps[t, own]

    maps[1] = mapped(cost_s, potential, row_lse(cost_s, potential), all_t)
    send_back(1)
    for m in range(nr):
        source_row[m * own_blocks : (m + 1) * own_blocks, :] = parts[
            ITERS - 1, m, blocks : blocks + own_blocks, :
        ]
    own_norm = [to_column(sums[pl.ds(me * own_blocks + b, 1), :]) for b in range(own_blocks)]
    maps[0] = mapped(cost_t, source_row, own_norm, all_s)
    send_back(0)

    for copy in line_copies + sent_copies + part_copies:
        copy.wait_send()

    def out_of_slots(t, ordering):
        for d in range(1, nc):
            back_copy(t, d).wait()
        return lax.dot_general(
            selector(ordering), back[t], (((0,), (0,)), ((), ())), preferred_element_type=jnp.float32
        ).astype(jnp.bfloat16)

    source_out[...] = out_of_slots(1, source_order)
    target_out[...] = out_of_slots(0, target_order)


def solution(mesh):
    nc, nr = mesh.shape["cluster"], mesh.shape["row"]

    def shards(sources, targets, source_order, target_order):
        rows, width = sources.shape
        columns = rows * nr
        blocks = columns // LANES
        own_blocks = rows // LANES
        nx, q = nc // CORES, nr // nc
        chunks = min(nc, 4)
        copies = chunks * max(
            a + b - 1 + (a - 1) * b + a * (b - 1) for a, b in ((nx, q), (q, nx))
        )
        vmem = pl.BlockSpec(memory_space=pltpu.VMEM)
        out = jax.ShapeDtypeStruct((rows, width), jnp.bfloat16)
        dma = pltpu.SemaphoreType.DMA
        return pl.pallas_call(
            functools.partial(kernel, nc, nr),
            out_shape=(out, out),
            in_specs=[vmem] * 4,
            out_specs=(vmem, vmem),
            scratch_shapes=[
                pltpu.VMEM((columns, width), jnp.bfloat16),
                pltpu.VMEM((columns, width), jnp.bfloat16),
                pltpu.VMEM((2, rows, width), jnp.bfloat16),
                pltpu.VMEM((2, rows, width), jnp.bfloat16),
                pltpu.VMEM((2, rows, width), jnp.bfloat16),
                pltpu.VMEM((rows, columns), jnp.float32),
                pltpu.VMEM((rows, columns), jnp.float32),
                pltpu.VMEM((blocks, LANES), jnp.float32),
                pltpu.VMEM((blocks, LANES), jnp.float32),
                pltpu.VMEM((blocks, LANES), jnp.float32),
                pltpu.VMEM((blocks, LANES), jnp.float32),
                pltpu.VMEM((ITERS, nr, blocks + 8, LANES), jnp.float32),
                dma((2, nc)), dma((2, nc)), dma((2, nc)), dma((2, nc)),
                dma((2, copies)), dma((2, chunks, nr)),
                dma((ITERS, nr)), dma((ITERS, nr)),
            ],
            compiler_params=pltpu.CompilerParams(
                collective_id=0, has_side_effects=True, vmem_limit_bytes=48 * 1024 * 1024
            ),
        )(sources, targets, source_order.reshape(1, rows), target_order.reshape(1, rows))

    return jax.shard_map(
        shards,
        mesh=mesh,
        in_specs=(
            P(("cluster", "row"), None),
            P(("cluster", "row"), None),
            P(("cluster", "row")),
            P(("cluster", "row")),
        ),
        out_specs=(P(("cluster", "row"), None), P(("cluster", "row"), None)),
        check_vma=False,
    )
```

time: 283 us -> 59.1 us (0.21)
  blocking collectives: 139 us -> 0 us
  matrix products: 55.1 us -> 0 us
  Pallas kernels: 0 us -> 54.3 us
  waiting for transfers between devices: 48.3 us -> 0 us
  between operations: 14.5 us -> 0.66 us
  starting transfers between devices: 10.3 us -> 0 us
  other arithmetic: 10 us -> 0 us
    pmax x3 -> x0, blocking collectives: 57.9 us -> none  [column_lse(): highest = lax.pmax(peaks, 'row')]
    dot_general x37 -> x0, matrix products: 55.1 us -> none  [the longest x28 39.7 us: cost_panel(): jnp.einsum('id,jd->ij', source_rows, target_rows, preferred_element_type=...]
    pallas_call x0 -> x1, Pallas kernels: none -> 54.3 us  [shards(): pl.pallas_call(functools.partial(kernel, nc, nr), out_shape=(out, out), i...]
    psum x3 -> x0, blocking collectives: 53.1 us -> none  [column_lse(): summed = lax.psum(totals * jnp.exp(peaks - highest), 'row')]
    all_gather x2 -> x0, waiting for transfers between devices: 37.4 us -> none  [the longest x1 37.4 us: shards(): cluster_targets = lax.all_gather(local_targets, 'row', axis=0, tiled=True)]
    all_gather x1 -> x0, blocking collectives: 18.2 us -> none  [shards(): lax.all_gather(source_potential, 'row', axis=0, tiled=True)]
    all_to_all x3 -> x0, waiting for transfers between devices: 10.9 us -> none  [the longest x1 5.86 us: shards(): lax.all_to_all(sent_sources, 'cluster', split_axis=0, concat_axis=0, tile...]
    all_to_all x3 -> x0, starting transfers between devices: 10.2 us -> none  [the longest x1 3.41 us: shards(): lax.all_to_all(target_map, 'cluster', split_axis=0, concat_axis=0, tiled=...]
  transfers between devices with their start and end apart: 5 -> 0, of which waited for: 3 -> 0; matrix products, arithmetic and copies ran while one was open for 23% -> 0% of each run, Pallas kernels for 0% -> 0%
where the time goes in v1:
time: 59.1 us; the launch traced here: 58.9 us
  Pallas kernels  54.3 us (92%)
  local copies, waits for them, and re-layouts  3.99 us (7%)
  between operations  0.66 us (1%)
    pallas_call x1, Pallas kernels, shards(): pl.pallas_call(functools.partial(kernel, nc, nr), out_shape=(out, out), i...  54.3 us
    unnamed x10, local copies, waits for them, and re-layouts  3.99 us

profile of v1, /device:TPU:0, one launch (start us, length us, event | category | flops | bytes accessed | tf_op | source)
XLA Modules:
  0.0 58.9 jit_solution(5071700582970139565)
XLA Ops:
  0.6 0.0 copy-start.3
  0.6 0.0 copy-start.2
  0.7 0.7 %copy-done.3 = s32[256]{0:T(256)S(1)} copy-done((s32[256]{0:T(256)S(1)}, s32[256]{0:T(256)}, u32[]{:S(2)}) %copy-start.3) | copy-done | bytes 1048
  1.3 0.0 copy-done.2
  1.3 0.0 copy-start
  1.3 0.9 %copy-done = bf16[256,512]{1,0:T(8,128)(2,1)S(1)} copy-done((bf16[256,512]{1,0:T(8,128)(2,1)S(1)}, bf16[256,512]{1,0:T(8,128)(2,1)}, u32[]{:S(2)}) %copy-start) | copy-done | bytes 262168
  2.3 0.0 copy-start.1
  2.3 0.9 %copy-done.1 = bf16[256,512]{1,0:T(8,128)(2,1)S(1)} copy-done((bf16[256,512]{1,0:T(8,128)(2,1)S(1)}, bf16[256,512]{1,0:T(8,128)(2,1)}, u32[]{:S(2)}) %copy-start.1) | copy-done | bytes 262168
  3.2 54.3 %shard_map.59 = (bf16[256,512]{1,0:T(8,128)(2,1)S(1)}, bf16[256,512]{1,0:T(8,128)(2,1)S(1)}) custom-call(bf16[256,512]{1,0:T(8,128)(2,1)S(1)} %copy-done, bf16[256,512]{1,0:T(8,128)(2,1)S(1)} %copy-done.1, s32[1,256]{1,0:T(1,128)S(1)} %bitcast.2, s32[1,256]{1,0:T(1,128)S(1)} %bitcast.3), custom_call_target="tpu_custom_call" | custom-call | tf_op jit(solution)/shard_map/pallas_call | solution.py:381
  57.5 0.7 %copy.8 = bf16[256,512]{1,0:T(8,128)(2,1)} copy(bf16[256,512]{1,0:T(8,128)(2,1)S(1)} %get-tuple-element.4) | data formatting | bytes 524288
  58.2 0.7 %copy.9 = bf16[256,512]{1,0:T(8,128)(2,1)} copy(bf16[256,512]{1,0:T(8,128)(2,1)S(1)} %get-tuple-element.5) | data formatting | bytes 524288
Async XLA Ops:
  0.6 0.7 %copy-start.3 = (s32[256]{0:T(256)S(1)}, s32[256]{0:T(256)}, u32[]{:S(2)}) copy-start(s32[256]{0:T(256)} %param.7) | copy-start | bytes 3076
  0.6 0.7 %copy-start.2 = (s32[256]{0:T(256)S(1)}, s32[256]{0:T(256)}, u32[]{:S(2)}) copy-start(s32[256]{0:T(256)} %param.6) | copy-start | bytes 3076
  1.3 0.9 %copy-start = (bf16[256,512]{1,0:T(8,128)(2,1)S(1)}, bf16[256,512]{1,0:T(8,128)(2,1)}, u32[]{:S(2)}) copy-start(bf16[256,512]{1,0:T(8,128)(2,1)} %sources.1) | copy-start | bytes 786436
  2.3 0.9 %copy-start.1 = (bf16[256,512]{1,0:T(8,128)(2,1)S(1)}, bf16[256,512]{1,0:T(8,128)(2,1)}, u32[]{:S(2)}) copy-start(bf16[256,512]{1,0:T(8,128)(2,1)} %targets.1) | copy-start | bytes 786436

commit v2 on v1

--- a/solution.py
+++ b/solution.py
@@ -17,8 +17,8 @@
 
 def kernel(
     nc, nr, sources, targets, source_order, target_order, source_out, target_out,
-    all_s, all_t, sent, maps, back, cost_s, cost_t, potential, source_row, peaks, sums, parts,
-    out_send, out_recv, own_send, own_recv, gather_send, gather_recv, part_send, part_recv,
+    given, all_s, all_t, sent, maps, back, cost_s, cost_t, target_norms, potential, source_row,
+    peaks, sums, parts, in_sem, out_send, out_recv, own_send, own_recv, gather_send, gather_recv, part_send, part_recv,
 ):
     rows, width = sources.shape
     per = rows // nc
@@ -50,6 +50,12 @@
     def line(d):
         return lax.rem(k + d, nc)
 
+    reads = [
+        pltpu.make_async_copy(ref, given.at[t], in_sem.at[t]) for t, ref in enumerate((targets, sources))
+    ]
+    for read in reads:
+        read.start()
+
     barrier = pltpu.get_barrier_semaphore()
     for d in range(1, nc):
         pl.semaphore_signal(barrier, inc=1, device_id=(c, line(d) * q + y), device_id_type=MESH)
@@ -66,30 +72,31 @@
         positions = lax.broadcasted_iota(jnp.int32, (rows, rows), 0)
         return (positions == ordering[...]).astype(jnp.float32).astype(jnp.bfloat16)
 
-    def own_rows(t, block, size):
-        return alls[t].at[pl.ds(pl.multiple_of(me * rows + block * size, size), size)]
-
-    def into_slots(t, ordering, matrix):
-        slots = jnp.dot(selector(ordering), matrix[...], preferred_element_type=jnp.float32)
+    def own_rows(t, block, owner=me):
+        return alls[t].at[pl.ds(pl.multiple_of(owner * rows + block * per, per), per)]
+
+    def into_slots(t, ordering):
+        reads[t].wait()
+        slots = jnp.dot(selector(ordering), given[t], preferred_element_type=jnp.float32)
         sent[t] = slots.astype(jnp.bfloat16)
-        own_rows(t, k, per)[...] = sent[t, pl.ds(pl.multiple_of(k * per, per), per)]
+        own_rows(t, 0)[...] = sent[t, pl.ds(pl.multiple_of(k * per, per), per)]
 
     def line_copy(t, d):
         return pltpu.make_async_remote_copy(
             src_ref=sent.at[t, pl.ds(pl.multiple_of(line(d) * per, per), per)],
-            dst_ref=own_rows(t, k, per),
+            dst_ref=own_rows(t, nc - d),
             send_sem=own_send.at[t, d],
             recv_sem=own_recv.at[t, d],
             device_id=(c, line(d) * q + y),
             device_id_type=MESH,
         )
 
-    into_slots(0, target_order, targets)
+    into_slots(0, target_order)
     pl.semaphore_wait(barrier, nc - 1 + nr - 1)
     line_copies = []
     for t in range(2):
         if t == 1:
-            into_slots(1, source_order, sources)
+            into_slots(1, source_order)
         for d in range(1, nc):
             copy = line_copy(t, d)
             copy.start()
@@ -99,7 +106,7 @@
     counts = [0, 0]
 
     def chunk_rows(t, i, owner):
-        start = owner * rows + lax.rem(k // group + i, chunks) * span
+        start = owner * rows + i * span
         return alls[t].at[pl.ds(pl.multiple_of(start, span), span)]
 
     def forward(t, i, owner, target):
@@ -137,24 +144,23 @@
     sibling_core = CORES - 1 - core
     sibling = (x, sibling_core, y)
 
-    def gather_own(t):
-        if group > 1:
-            for d in range(1, nc):
-                line_copy(t, d).wait_recv()
+    def gather_own(t, after=None):
         for i in range(chunks):
-            if group == 1 and i > 0:
-                d = nc - i
-                pltpu.make_async_remote_copy(
-                    src_ref=sent.at[t, pl.ds(0, per)], dst_ref=own_rows(t, line(i), per),
-                    send_sem=own_send.at[t, d], recv_sem=own_recv.at[t, d],
-                    device_id=(c, line(i) * q + y), device_id_type=MESH,
-                ).wait_recv()
+            for j in range(i * group, (i + 1) * group):
+                if j > 0:
+                    pltpu.make_async_remote_copy(
+                        src_ref=sent.at[t, pl.ds(0, per)], dst_ref=own_rows(t, j),
+                        send_sem=own_send.at[t, nc - j], recv_sem=own_recv.at[t, nc - j],
+                        device_id=(c, line(j) * q + y), device_id_type=MESH,
+                    ).wait_recv()
             first, second = axes(i)
             for step in range(1, first):
                 forward(t, i, here, at(along(i, step, 0)))
             for step in range(1, second):
                 forward(t, i, here, at(along(i, 0, step)))
             forward(t, i, here, sibling)
+            if after is not None:
+                after((i + 1) * span)
 
     def gather_first(t):
         for i in range(chunks):
@@ -198,42 +204,64 @@
     def shard(ref, owner):
         return ref[pl.ds(pl.multiple_of(owner * rows, rows), rows)]
 
-    def build(out, own_ref, all_ref, owners):
-        own = shard(own_ref, me)
+    def norms_row(matrix):
+        norms = square_sums(matrix)
+        return [to_row(norms[b * LANES : (b + 1) * LANES]) for b in range(own_blocks)]
+
+    def build_sources(part):
+        own = all_s[pl.ds(pl.multiple_of(me * rows + part * LANES, LANES), LANES)]
         own_norms = square_sums(own)
+        for m in range(nr):
+            inner = lax.dot_general(
+                own, all_t[m * rows : (m + 1) * rows, :], (((1,), (1,)), ((), ())),
+                preferred_element_type=jnp.float32,
+            )
+            for b in range(own_blocks):
+                block = m * own_blocks + b
+                cost_s[part * LANES : (part + 1) * LANES, block * LANES : (block + 1) * LANES] = scale * (
+                    2.0 * inner[:, b * LANES : (b + 1) * LANES]
+                    - own_norms - target_norms[block : block + 1, :]
+                )
+
+    def build_targets(which):
+        own = shard(all_t, me)
+        own_norms = square_sums(own)
 
         def panel(index, _):
-            owner = owners(index)
-            other = shard(all_ref, owner)
+            owner = member(index // q, which, lax.rem(index, q))
+            other = shard(all_s, owner)
             inner = lax.dot_general(
                 own, other, (((1,), (1,)), ((), ())), preferred_element_type=jnp.float32
             )
-            norms = square_sums(other)
-            norms = jnp.concatenate(
-                [to_row(norms[b * LANES : (b + 1) * LANES]) for b in range(own_blocks)], axis=1
-            )
-            out[:, pl.ds(pl.multiple_of(owner * rows, rows), rows)] = scale * (
+            norms = jnp.concatenate(norms_row(other), axis=1)
+            cost_t[:, pl.ds(pl.multiple_of(owner * rows, rows), rows)] = scale * (
                 2.0 * inner - own_norms - norms
             )
             return 0
 
-        return panel
-
-    def row_lse(cost, row):
-        norms = []
-        for h in range(own_blocks):
-            part = pl.ds(h * LANES, LANES)
-            peak = None
-            for b in range(blocks):
-                scores = cost[part, b * LANES : (b + 1) * LANES] + row[b : b + 1, :]
-                peak = scores if peak is None else jnp.maximum(peak, scores)
-            peak = jnp.max(peak, axis=1, keepdims=True)
-            total = jnp.zeros((LANES, LANES), jnp.float32)
-            for b in range(blocks):
-                scores = cost[part, b * LANES : (b + 1) * LANES] + row[b : b + 1, :]
-                total = total + jnp.exp2(scores - peak)
-            norms.append(peak + jnp.log2(jnp.sum(total, axis=1, keepdims=True)))
-        return norms
+        lax.fori_loop(0, nx * q, panel, 0)
+
+    def norm_targets(which):
+        def panel(index, _):
+            owner = member(index // q, which, lax.rem(index, q))
+            for b, norms in enumerate(norms_row(shard(all_t, owner))):
+                target_norms[pl.ds(owner * own_blocks + b, 1), :] = norms
+            return 0
+
+        lax.fori_loop(0, nx * q, panel, 0)
+
+    def row_lse(cost, row, h):
+        part = pl.ds(h * LANES, LANES)
+        peak = None
+        for b in range(blocks):
+            scores = cost[part, b * LANES : (b + 1) * LANES] + row[b : b + 1, :]
+            peak = scores if peak is None else jnp.maximum(peak, scores)
+        peak = jnp.max(peak, axis=1, keepdims=True)
+        total = jnp.zeros((LANES, LANES), jnp.float32)
+        for b in range(blocks):
+            scores = cost[part, b * LANES : (b + 1) * LANES] + row[b : b + 1, :]
+            total = total + jnp.exp2(scores - peak)
+        return peak + jnp.log2(jnp.sum(total, axis=1, keepdims=True))
 
     def column_lse(cost, column):
         for b in range(blocks):
@@ -243,15 +271,15 @@
             sums[b : b + 1, :] = jnp.sum(jnp.exp2(scores - peak), axis=0, keepdims=True)
         return peaks[...] + jnp.log2(sums[...])
 
-    def mapped(cost, row, norms, all_ref):
-        norms = jnp.concatenate(norms, axis=0)
-        total = jnp.zeros((rows, width), jnp.float32)
+    def mapped(cost, row, norm, all_ref, h):
+        part = pl.ds(h * LANES, LANES)
+        total = jnp.zeros((LANES, width), jnp.float32)
         step = 4 * LANES
         for start in range(0, columns, step):
             pieces = []
             for b in range(start // LANES, (start + step) // LANES):
-                scores = cost[:, b * LANES : (b + 1) * LANES] + row[b : b + 1, :]
-                pieces.append(jnp.exp2(scores - norms).astype(jnp.bfloat16))
+                scores = cost[part, b * LANES : (b + 1) * LANES] + row[b : b + 1, :]
+                pieces.append(jnp.exp2(scores - norm).astype(jnp.bfloat16))
             total = total + jnp.dot(
                 jnp.concatenate(pieces, axis=1),
                 all_ref[start : start + step, :],
@@ -262,22 +290,29 @@
     gather_own(0)
     gather_first(0)
     gather_second(0)
-    gather_own(1)
-    panel = build(cost_s, all_s, all_t, lambda index: member(
-        index // q, core, lax.rem(index, q)))
-    lax.fori_loop(0, nx * q, panel, 0)
+    norm_targets(core)
     for dx in range(nx):
         for dy in range(q):
             gather_sibling(0, at((dx, dy), sibling_core))
-    panel = build(cost_s, all_s, all_t, lambda index: member(
-        index // q, sibling_core, lax.rem(index, q)))
-    lax.fori_loop(0, nx * q, panel, 0)
+    norm_targets(sibling_core)
 
     potential[...] = jnp.zeros_like(potential)
+    first_norms = []
+
+    def first_rows(arrived):
+        while len(first_norms) < arrived // LANES:
+            build_sources(len(first_norms))
+            first_norms.append(row_lse(cost_s, potential, len(first_norms)))
+
+    gather_own(1, first_rows)
     part_copies = []
     for repeat in range(ITERS):
         last = repeat == ITERS - 1
-        source_potential = [log_mass - norm for norm in row_lse(cost_s, potential)]
+        if repeat == 0:
+            norms = first_norms
+        else:
+            norms = [row_lse(cost_s, potential, h) for h in range(own_blocks)]
+        source_potential = [log_mass - norm for norm in norms]
         mine = column_lse(cost_s, jnp.concatenate(source_potential, axis=0))
         parts[repeat, me, 0:blocks, :] = mine
         used = blocks
@@ -300,11 +335,12 @@
             gather_first(1)
         if repeat == 1:
             gather_second(1)
+            build_targets(core)
         if last:
             for dx in range(nx):
                 for dy in range(q):
                     gather_sibling(1, at((dx, dy), sibling_core))
-            lax.fori_loop(0, nr, build(cost_t, all_t, all_s, lambda index: index), 0)
+            build_targets(sibling_core)
         for number, other in enumerate(others):
             owner = member(*other)
             pltpu.make_async_remote_copy(
@@ -324,7 +360,7 @@
 
     def back_copy(t, d):
         return pltpu.make_async_remote_copy(
-            src_ref=maps.at[t, pl.ds(pl.multiple_of(line(d) * per, per), per)],
+            src_ref=maps.at[t, d * per : (d + 1) * per],
             dst_ref=back.at[t, pl.ds(pl.multiple_of(k * per, per), per)],
             send_sem=out_send.at[t, d],
             recv_sem=out_recv.at[t, d],
@@ -332,21 +368,24 @@
             device_id_type=MESH,
         )
 
-    def send_back(t):
-        for d in range(1, nc):
-            back_copy(t, d).start()
-        own = pl.ds(pl.multiple_of(k * per, per), per)
-        back[t, own] = maps[t, own]
-
-    maps[1] = mapped(cost_s, potential, row_lse(cost_s, potential), all_t)
-    send_back(1)
+    def send_back(t, h, result):
+        maps[t, h * LANES : (h + 1) * LANES] = result
+        for d in range(h * LANES // per, (h + 1) * LANES // per):
+            if d > 0:
+                back_copy(t, d).start()
+            else:
+                back[t, pl.ds(pl.multiple_of(k * per, per), per)] = maps[t, 0:per]
+
     for m in range(nr):
         source_row[m * own_blocks : (m + 1) * own_blocks, :] = parts[
             ITERS - 1, m, blocks : blocks + own_blocks, :
         ]
-    own_norm = [to_column(sums[pl.ds(me * own_blocks + b, 1), :]) for b in range(own_blocks)]
-    maps[0] = mapped(cost_t, source_row, own_norm, all_s)
-    send_back(0)
+    for h in reversed(range(own_blocks)):
+        norm = to_column(sums[pl.ds(me * own_blocks + h, 1), :])
+        send_back(0, h, mapped(cost_t, source_row, norm, all_s, h))
+    for h in reversed(range(own_blocks)):
+        norm = row_lse(cost_s, potential, h)
+        send_back(1, h, mapped(cost_s, potential, norm, all_t, h))
 
     for copy in line_copies + sent_copies + part_copies:
         copy.wait_send()
@@ -358,8 +397,14 @@
             selector(ordering), back[t], (((0,), (0,)), ((), ())), preferred_element_type=jnp.float32
         ).astype(jnp.bfloat16)
 
-    source_out[...] = out_of_slots(1, source_order)
-    target_out[...] = out_of_slots(0, target_order)
+    writes = []
+    for t, (ordering, out) in enumerate(((target_order, target_out), (source_order, source_out))):
+        given[t] = out_of_slots(t, ordering)
+        write = pltpu.make_async_copy(given.at[t], out, in_sem.at[t])
+        write.start()
+        writes.append(write)
+    for write in writes:
+        write.wait()
 
 
 def solution(mesh):
@@ -381,9 +426,10 @@
         return pl.pallas_call(
             functools.partial(kernel, nc, nr),
             out_shape=(out, out),
-            in_specs=[vmem] * 4,
-            out_specs=(vmem, vmem),
+            in_specs=[pl.BlockSpec(memory_space=pl.ANY)] * 2 + [vmem] * 2,
+            out_specs=(pl.BlockSpec(memory_space=pl.ANY),) * 2,
             scratch_shapes=[
+                pltpu.VMEM((2, rows, width), jnp.bfloat16),
                 pltpu.VMEM((columns, width), jnp.bfloat16),
                 pltpu.VMEM((columns, width), jnp.bfloat16),
                 pltpu.VMEM((2, rows, width), jnp.bfloat16),
@@ -395,13 +441,14 @@
                 pltpu.VMEM((blocks, LANES), jnp.float32),
                 pltpu.VMEM((blocks, LANES), jnp.float32),
                 pltpu.VMEM((blocks, LANES), jnp.float32),
+                pltpu.VMEM((blocks, LANES), jnp.float32),
                 pltpu.VMEM((ITERS, nr, blocks + 8, LANES), jnp.float32),
-                dma((2, nc)), dma((2, nc)), dma((2, nc)), dma((2, nc)),
+                dma((2,)), dma((2, nc)), dma((2, nc)), dma((2, nc)), dma((2, nc)),
                 dma((2, copies)), dma((2, chunks, nr)),
                 dma((ITERS, nr)), dma((ITERS, nr)),
             ],
             compiler_params=pltpu.CompilerParams(
-                collective_id=0, has_side_effects=True, vmem_limit_bytes=48 * 1024 * 1024
+                collective_id=0, has_side_effects=True, vmem_limit_bytes=63 * 1024 * 1024
             ),
         )(sources, targets, source_order.reshape(1, rows), target_order.reshape(1, rows))
 

time: 59.1 us -> 61.1 us (1.034)
  Pallas kernels: 54.3 us -> 57.9 us
  local copies, waits for them, and re-layouts: 3.99 us -> 2.42 us
    pallas_call x1, Pallas kernels: 54.3 us -> 57.9 us  [shards(): pl.pallas_call(functools.partial(kernel, nc, nr), out_shape=(out, out), i...]
    unnamed x10 -> x4, local copies, waits for them, and re-layouts: 3.99 us -> 2.42 us
where the time goes in v2:
time: 61.1 us; the launch traced here: 60.9 us
  Pallas kernels  57.9 us (95%)
  local copies, waits for them, and re-layouts  2.42 us (4%)
  between operations  0.65 us (1%)
    pallas_call x1, Pallas kernels, shards(): pl.pallas_call(functools.partial(kernel, nc, nr), out_shape=(out, out), i...  57.9 us
    unnamed x4, local copies, waits for them, and re-layouts  2.42 us

profile of v2, /device:TPU:0, one launch (start us, length us, event | category | flops | bytes accessed | tf_op | source)
XLA Modules:
  0.0 60.9 jit_solution(8497605872934626918)
XLA Ops:
  0.6 57.9 %shard_map.59 = (bf16[256,512]{1,0:T(8,128)(2,1)}, bf16[256,512]{1,0:T(8,128)(2,1)}) custom-call(bf16[256,512]{1,0:T(8,128)(2,1)} %sources.1, bf16[256,512]{1,0:T(8,128)(2,1)} %targets.1, s32[1,256]{1,0:T(1,128)} %bitcast.2, s32[1,256]{1,0:T(1,128)} %bitcast.3), custom_call_target="tpu_custom_call" | custom-call | tf_op jit(solution)/shard_map/pallas_call | solution.py:426
  58.5 0.0 copy-start
  58.5 1.7 %copy.8 = bf16[256,512]{1,0:T(8,128)(2,1)} copy(bf16[256,512]{1,0:T(8,128)(2,1)} %get-tuple-element.4) | data formatting | bytes 524288
  60.2 0.0 copy-done
  60.2 0.7 %copy.9 = bf16[256,512]{1,0:T(8,128)(2,1)} copy(bf16[256,512]{1,0:T(8,128)(2,1)S(1)} %copy-done) | data formatting | bytes 524288
Async XLA Ops:
  58.5 1.7 %copy-start = (bf16[256,512]{1,0:T(8,128)(2,1)S(1)}, bf16[256,512]{1,0:T(8,128)(2,1)}, u32[]{:S(2)}) copy-start(bf16[256,512]{1,0:T(8,128)(2,1)} %get-tuple-element.5) | copy-start | bytes 786436

commit v3 on v2

v3 whole, which is shorter than its diff:
```python
import functools
import math

import jax
import jax.numpy as jnp
from jax import lax
from jax.experimental import pallas as pl
from jax.experimental.pallas import tpu as pltpu
from jax.sharding import PartitionSpec as P

ITERS = 3
entropy_weight = 0.02
LANES = 128
CORES = 2
MESH = pl.DeviceIdType.MESH


def kernel(
    nc, nr, sources, targets, source_order, target_order, source_out, target_out,
    given, alls, sent, maps, back, cost, square_rows, potentials, norms, peaks, sums, parts,
    in_sem, out_send, out_recv, own_send, own_recv, gather_send, gather_recv, part_send, part_recv,
):
    rows, width = sources.shape
    per = rows // nc
    q = nr // nc
    nx = nc // CORES
    columns = alls.shape[1]
    blocks = columns // LANES
    own_blocks = rows // LANES
    chunks = min(nc, 4)
    group = nc // chunks
    span = rows // chunks
    log_mass = -math.log2(columns)
    scale = math.log2(math.e) / (width * entropy_weight)

    c = lax.axis_index("cluster")
    r = lax.axis_index("row")
    x, core = c // CORES, c % CORES
    k, y = r // q, r % q

    def member(mx, mcore, my):
        return (mx * CORES + mcore) * q + my

    def device(mx, mcore, my):
        return (mx * CORES + mcore, k * q + my)

    me = member(x, core, y)

    def line(d):
        return lax.rem(k + d, nc)

    reads = [
        pltpu.make_async_copy(ref, given.at[t], in_sem.at[t]) for t, ref in enumerate((targets, sources))
    ]
    for read in reads:
        read.start()

    barrier = pltpu.get_barrier_semaphore()
    for d in range(1, nc):
        pl.semaphore_signal(barrier, inc=1, device_id=(c, line(d) * q + y), device_id_type=MESH)
    others = []
    for dx in range(nx):
        for dcore in range(CORES):
            for dy in range(q):
                if dx or dcore or dy:
                    others.append((lax.rem(x + dx, nx), lax.rem(core + dcore, CORES), lax.rem(y + dy, q)))
    for other in others:
        pl.semaphore_signal(barrier, inc=1, device_id=device(*other), device_id_type=MESH)

    def selector(ordering):
        positions = lax.broadcasted_iota(jnp.int32, (rows, rows), 0)
        return (positions == ordering[...]).astype(jnp.float32).astype(jnp.bfloat16)

    def own_rows(t, block, owner=me):
        return alls.at[t, pl.ds(pl.multiple_of(owner * rows + block * per, per), per)]

    def into_slots(t, ordering):
        reads[t].wait()
        slots = jnp.dot(selector(ordering), given[t], preferred_element_type=jnp.float32)
        sent[t] = slots.astype(jnp.bfloat16)
        own_rows(t, 0)[...] = sent[t, pl.ds(pl.multiple_of(k * per, per), per)]

    def line_copy(t, d):
        return pltpu.make_async_remote_copy(
            src_ref=sent.at[t, pl.ds(pl.multiple_of(line(d) * per, per), per)],
            dst_ref=own_rows(t, nc - d),
            send_sem=own_send.at[t, d],
            recv_sem=own_recv.at[t, d],
            device_id=(c, line(d) * q + y),
            device_id_type=MESH,
        )

    into_slots(0, target_order)
    pl.semaphore_wait(barrier, nc - 1 + nr - 1)
    line_copies = []
    for t in range(2):
        if t == 1:
            into_slots(1, source_order)
        for d in range(1, nc):
            copy = line_copy(t, d)
            copy.start()
            line_copies.append(copy)

    counts = [0, 0]

    def chunk_rows(t, i, owner):
        start = owner * rows + i * span
        return alls.at[t, pl.ds(pl.multiple_of(start, span), span)]

    def forward(t, i, owner, target):
        number = counts[t]
        counts[t] += 1
        owner = member(*owner)
        where = chunk_rows(t, i, owner)
        copy = pltpu.make_async_remote_copy(
            src_ref=where, dst_ref=where,
            send_sem=gather_send.at[t, number], recv_sem=gather_recv.at[t, i, owner],
            device_id=device(*target), device_id_type=MESH,
        )
        copy.start()

    def arrive(t, i, owner):
        owner = member(*owner)
        where = chunk_rows(t, i, owner)
        pltpu.make_async_remote_copy(
            src_ref=where, dst_ref=where,
            send_sem=gather_send.at[t, 0], recv_sem=gather_recv.at[t, i, owner],
            device_id=device(*others[0]), device_id_type=MESH,
        ).wait_recv()

    def along(i, first, second):
        return (first, second) if i % 2 == 0 else (second, first)

    def at(step, on=None):
        return (lax.rem(x + step[0], nx), core if on is None else on, lax.rem(y + step[1], q))

    def axes(i):
        return (nx, q) if i % 2 == 0 else (q, nx)

    here = (x, core, y)
    sibling_core = CORES - 1 - core
    sibling = (x, sibling_core, y)

    def gather_own(t):
        for i in range(chunks):
            for j in range(i * group, (i + 1) * group):
                if j > 0:
                    pltpu.make_async_remote_copy(
                        src_ref=sent.at[t, pl.ds(0, per)], dst_ref=own_rows(t, j),
                        send_sem=own_send.at[t, nc - j], recv_sem=own_recv.at[t, nc - j],
                        device_id=(c, line(j) * q + y), device_id_type=MESH,
                    ).wait_recv()
            first, second = axes(i)
            for step in range(1, first):
                forward(t, i, here, at(along(i, step, 0)))
            for step in range(1, second):
                forward(t, i, here, at(along(i, 0, step)))
            forward(t, i, here, sibling)

    def gather_first(t):
        for i in range(chunks):
            first, second = axes(i)
            for step in range(1, first):
                owner = at(along(i, step, 0))
                arrive(t, i, owner)
                for turn in range(1, second):
                    forward(t, i, owner, at(along(i, 0, turn)))
                forward(t, i, owner, sibling)

    def gather_second(t):
        for i in range(chunks):
            first, second = axes(i)
            for step in range(first):
                for turn in range(1, second):
                    owner = at(along(i, step, turn))
                    arrive(t, i, owner)
                    forward(t, i, owner, sibling)

    def gather_sibling(t, owner):
        for i in range(chunks):
            arrive(t, i, owner)

    diagonal = lax.broadcasted_iota(jnp.int32, (LANES, LANES), 0) == lax.broadcasted_iota(
        jnp.int32, (LANES, LANES), 1
    )

    def to_row(column):
        spread = jnp.broadcast_to(column, (LANES, LANES))
        return jnp.sum(jnp.where(diagonal, spread, 0.0), axis=0, keepdims=True)

    def to_column(row):
        spread = jnp.broadcast_to(row, (LANES, LANES))
        return jnp.sum(jnp.where(diagonal, spread, 0.0), axis=1, keepdims=True)

    def square_sums(matrix):
        widened = matrix.astype(jnp.float32)
        return jnp.sum(widened * widened, axis=1, keepdims=True)

    def shard(t, owner):
        return alls[t, pl.ds(pl.multiple_of(owner * rows, rows), rows)]

    def over_members(which, body):
        def step(index, _):
            body(member(index // q, which, lax.rem(index, q)))
            return 0

        lax.fori_loop(0, nx * q, step, 0)

    def square_panels(t, which):
        def panel(owner):
            squares = square_sums(shard(t, owner))
            for b in range(own_blocks):
                square_rows[t, pl.ds(owner * own_blocks + b, 1), :] = to_row(
                    squares[b * LANES : (b + 1) * LANES]
                )

        over_members(which, panel)

    def build(t, which):
        own = shard(t, me)
        own_squares = square_sums(own)

        def panel(owner):
            inner = lax.dot_general(
                own, shard(1 - t, owner), (((1,), (1,)), ((), ())),
                preferred_element_type=jnp.float32,
            )
            squares = jnp.concatenate(
                [square_rows[1 - t, pl.ds(owner * own_blocks + b, 1), :] for b in range(own_blocks)],
                axis=1,
            )
            cost[t, :, pl.ds(pl.multiple_of(owner * rows, rows), rows)] = scale * (
                2.0 * inner - own_squares - squares
            )

        over_members(which, panel)

    def row_pass():
        def half(h, _):
            part = pl.ds(pl.multiple_of(h * LANES, LANES), LANES)

            def scores(b):
                return cost[1, part, b * LANES : (b + 1) * LANES] + potentials[1, b : b + 1, :]

            peak = functools.reduce(jnp.maximum, (scores(b) for b in range(blocks)))
            peak = jnp.max(peak, axis=1, keepdims=True)
            total = jnp.zeros((LANES, LANES), jnp.float32)
            for b in range(blocks):
                total = total + jnp.exp2(scores(b) - peak)
            norm = peak + jnp.log2(jnp.sum(total, axis=1, keepdims=True))
            norms[1, part, :] = jnp.broadcast_to(norm, (LANES, LANES))
            return 0

        lax.fori_loop(0, own_blocks, half, 0)

    def column_pass():
        def block(b, _):
            lanes = pl.ds(pl.multiple_of(b * LANES, LANES), LANES)
            scores = cost[1, :, lanes] + (log_mass - norms[1])
            peak = jnp.max(scores, axis=0, keepdims=True)
            peaks[pl.ds(b, 1), :] = peak
            sums[pl.ds(b, 1), :] = jnp.sum(jnp.exp2(scores - peak), axis=0, keepdims=True)
            return 0

        lax.fori_loop(0, blocks, block, 0, unroll=2)
        return peaks[...] + jnp.log2(sums[...])

    def part_copy(repeat, number, owner):
        where = parts.at[repeat, owner, pl.ds(0, blocks + own_blocks)]
        return pltpu.make_async_remote_copy(
            src_ref=where,
            dst_ref=where,
            send_sem=part_send.at[repeat, number],
            recv_sem=part_recv.at[repeat, owner],
            device_id=device(*others[number]),
            device_id_type=MESH,
        )

    gather_own(0)
    gather_first(0)
    gather_second(0)
    square_panels(0, core)
    for dx in range(nx):
        for dy in range(q):
            gather_sibling(0, at((dx, dy), sibling_core))
    square_panels(0, sibling_core)
    gather_own(1)
    build(1, core)
    build(1, sibling_core)

    potentials[1] = jnp.zeros_like(potentials[1])

    def iteration(repeat, _):
        row_pass()
        parts[repeat, me, 0:blocks, :] = column_pass()
        for b in range(own_blocks):
            parts[repeat, me, blocks + b : blocks + b + 1, :] = to_row(
                log_mass - norms[1, b * LANES : (b + 1) * LANES, :]
            )
        for number in range(len(others)):
            part_copy(repeat, number, me).start()

        @pl.when(repeat == 0)
        def _():
            gather_first(1)

        @pl.when(repeat == 1)
        def _():
            gather_second(1)
            square_panels(1, core)
            build(0, core)

        @pl.when(repeat == ITERS - 1)
        def _():
            for dx in range(nx):
                for dy in range(q):
                    gather_sibling(1, at((dx, dy), sibling_core))
            square_panels(1, sibling_core)
            build(0, sibling_core)

        for number, other in enumerate(others):
            part_copy(repeat, number, member(*other)).wait_recv()
        each = [parts[repeat, m, 0:blocks, :] for m in range(nr)]
        peak = functools.reduce(jnp.maximum, each)
        column_norm = peak + jnp.log2(sum(jnp.exp2(one - peak) for one in each))
        potentials[1] = log_mass - column_norm
        sums[...] = column_norm
        return 0

    lax.fori_loop(0, ITERS, iteration, 0)

    def back_copy(t, d):
        return pltpu.make_async_remote_copy(
            src_ref=maps.at[t, pl.ds(pl.multiple_of(d * per, per), per)],
            dst_ref=back.at[t, pl.ds(pl.multiple_of(k * per, per), per)],
            send_sem=out_send.at[t, d],
            recv_sem=out_recv.at[t, d],
            device_id=(c, line(d) * q + y),
            device_id_type=MESH,
        )

    for m in range(nr):
        potentials[0, m * own_blocks : (m + 1) * own_blocks, :] = parts[
            ITERS - 1, m, blocks : blocks + own_blocks, :
        ]
    for b in range(own_blocks):
        norms[0, b * LANES : (b + 1) * LANES, :] = jnp.broadcast_to(
            to_column(sums[pl.ds(me * own_blocks + b, 1), :]), (LANES, LANES)
        )

    def mapped(t, h):
        part = pl.ds(pl.multiple_of(h * LANES, LANES), LANES)
        total = jnp.zeros((LANES, width), jnp.float32)
        step = 4 * LANES
        for start in range(0, columns, step):
            pieces = []
            for b in range(start // LANES, (start + step) // LANES):
                scores = cost[t, part, b * LANES : (b + 1) * LANES] + potentials[t, b : b + 1, :]
                pieces.append(jnp.exp2(scores - norms[t, part, :]).astype(jnp.bfloat16))
            total = total + jnp.dot(
                jnp.concatenate(pieces, axis=1),
                alls[1 - t, start : start + step, :],
                preferred_element_type=jnp.float32,
            )
        maps[t, part] = total.astype(jnp.bfloat16)
        for j in range(LANES // per):
            d = h * (LANES // per) + j

            @pl.when(d > 0)
            def _():
                back_copy(t, d).start()

    def both_maps(t, _):
        @pl.when(t == 1)
        def _():
            row_pass()

        def half(j, _):
            mapped(t, own_blocks - 1 - j)
            return 0

        lax.fori_loop(0, own_blocks, half, 0)
        back[t, pl.ds(pl.multiple_of(k * per, per), per)] = maps[t, 0:per]
        return 0

    lax.fori_loop(0, 2, both_maps, 0)

    for copy in line_copies:
        copy.wait_send()
    for t in range(2):
        for number in range(counts[t]):
            pltpu.make_async_remote_copy(
                src_ref=chunk_rows(t, 0, me), dst_ref=chunk_rows(t, 0, me),
                send_sem=gather_send.at[t, number], recv_sem=gather_recv.at[t, 0, me],
                device_id=device(*others[0]), device_id_type=MESH,
            ).wait_send()
    for repeat in range(ITERS):
        for number in range(len(others)):
            part_copy(repeat, number, me).wait_send()

    def out_of_slots(t, ordering):
        for d in range(1, nc):
            back_copy(t, d).wait()
        return lax.dot_general(
            selector(ordering), back[t], (((0,), (0,)), ((), ())), preferred_element_type=jnp.float32
        ).astype(jnp.bfloat16)

    writes = []
    for t, (ordering, out) in enumerate(((target_order, target_out), (source_order, source_out))):
        given[t] = out_of_slots(t, ordering)
        write = pltpu.make_async_copy(given.at[t], out, in_sem.at[t])
        write.start()
        writes.append(write)
    for write in writes:
        write.wait()


def solution(mesh):
    nc, nr = mesh.shape["cluster"], mesh.shape["row"]

    def shards(sources, targets, source_order, target_order):
        rows, width = sources.shape
        columns = rows * nr
        blocks = columns // LANES
        own_blocks = rows // LANES
        nx, q = nc // CORES, nr // nc
        chunks = min(nc, 4)
        copies = chunks * max(
            a + b - 1 + (a - 1) * b + a * (b - 1) for a, b in ((nx, q), (q, nx))
        )
        vmem = pl.BlockSpec(memory_space=pltpu.VMEM)
        out = jax.ShapeDtypeStruct((rows, width), jnp.bfloat16)
        dma = pltpu.SemaphoreType.DMA
        return pl.pallas_call(
            functools.partial(kernel, nc, nr),
            out_shape=(out, out),
            in_specs=[pl.BlockSpec(memory_space=pl.ANY)] * 2 + [vmem] * 2,
            out_specs=(pl.BlockSpec(memory_space=pl.ANY),) * 2,
            scratch_shapes=[
                pltpu.VMEM((2, rows, width), jnp.bfloat16),
                pltpu.VMEM((2, columns, width), jnp.bfloat16),
                pltpu.VMEM((2, rows, width), jnp.bfloat16),
                pltpu.VMEM((2, rows, width), jnp.bfloat16),
                pltpu.VMEM((2, rows, width), jnp.bfloat16),
                pltpu.VMEM((2, rows, columns), jnp.float32),
                pltpu.VMEM((2, blocks, LANES), jnp.float32),
                pltpu.VMEM((2, blocks, LANES), jnp.float32),
                pltpu.VMEM((2, rows, LANES), jnp.float32),
                pltpu.VMEM((blocks, LANES), jnp.float32),
                pltpu.VMEM((blocks, LANES), jnp.float32),
                pltpu.VMEM((ITERS, nr, blocks + 8, LANES), jnp.float32),
                dma((2,)), dma((2, nc)), dma((2, nc)), dma((2, nc)), dma((2, nc)),
                dma((2, copies)), dma((2, chunks, nr)),
                dma((ITERS, nr)), dma((ITERS, nr)),
            ],
            compiler_params=pltpu.CompilerParams(
                collective_id=0, has_side_effects=True, vmem_limit_bytes=63 * 1024 * 1024
            ),
        )(sources, targets, source_order.reshape(1, rows), target_order.reshape(1, rows))

    return jax.shard_map(
        shards,
        mesh=mesh,
        in_specs=(
            P(("cluster", "row"), None),
            P(("cluster", "row"), None),
            P(("cluster", "row")),
            P(("cluster", "row")),
        ),
        out_specs=(P(("cluster", "row"), None), P(("cluster", "row"), None)),
        check_vma=False,
    )
```

time: 61.1 us -> 62.3 us (1.020)
  Pallas kernels: 57.9 us -> 59.1 us
    pallas_call x1, Pallas kernels: 57.9 us -> 59.1 us  [shards(): pl.pallas_call(functools.partial(kernel, nc, nr), out_shape=(out, out), i...]
where the time goes in v3:
time: 62.3 us; the launch traced here: 62.1 us
  Pallas kernels  59.1 us (95%)
  local copies, waits for them, and re-layouts  2.42 us (4%)
  between operations  0.65 us (1%)
    pallas_call x1, Pallas kernels, shards(): pl.pallas_call(functools.partial(kernel, nc, nr), out_shape=(out, out), i...  59.1 us
    unnamed x4, local copies, waits for them, and re-layouts  2.42 us

profile of v3, /device:TPU:0, one launch (start us, length us, event | category | flops | bytes accessed | tf_op | source)
XLA Modules:
  0.0 62.1 jit_solution(2866798900342674960)
XLA Ops:
  0.6 59.1 %shard_map.59 = (bf16[256,512]{1,0:T(8,128)(2,1)}, bf16[256,512]{1,0:T(8,128)(2,1)}) custom-call(bf16[256,512]{1,0:T(8,128)(2,1)} %sources.1, bf16[256,512]{1,0:T(8,128)(2,1)} %targets.1, s32[1,256]{1,0:T(1,128)} %bitcast.2, s32[1,256]{1,0:T(1,128)} %bitcast.3), custom_call_target="tpu_custom_call" | custom-call | tf_op jit(solution)/shard_map/pallas_call | solution.py:434
  59.7 0.0 copy-start
  59.7 1.7 %copy.8 = bf16[256,512]{1,0:T(8,128)(2,1)} copy(bf16[256,512]{1,0:T(8,128)(2,1)} %get-tuple-element.4) | data formatting | bytes 524288
  61.4 0.0 copy-done
  61.4 0.7 %copy.9 = bf16[256,512]{1,0:T(8,128)(2,1)} copy(bf16[256,512]{1,0:T(8,128)(2,1)S(1)} %copy-done) | data formatting | bytes 524288
Async XLA Ops:
  59.7 1.7 %copy-start = (bf16[256,512]{1,0:T(8,128)(2,1)S(1)}, bf16[256,512]{1,0:T(8,128)(2,1)}, u32[]{:S(2)}) copy-start(bf16[256,512]{1,0:T(8,128)(2,1)} %get-tuple-element.5) | copy-start | bytes 786436

commit v4 on v3

--- a/solution.py
+++ b/solution.py
@@ -17,8 +17,8 @@
 
 def kernel(
     nc, nr, sources, targets, source_order, target_order, source_out, target_out,
-    given, alls, sent, maps, back, cost, square_rows, potentials, norms, peaks, sums, parts,
-    in_sem, out_send, out_recv, own_send, own_recv, gather_send, gather_recv, part_send, part_recv,
+    alls, sent, maps, back, cost, square_rows, potentials, norms, peaks, sums, parts,
+    out_send, out_recv, own_send, own_recv, gather_send, gather_recv, part_send, part_recv,
 ):
     rows, width = sources.shape
     per = rows // nc
@@ -49,12 +49,6 @@
     def line(d):
         return lax.rem(k + d, nc)
 
-    reads = [
-        pltpu.make_async_copy(ref, given.at[t], in_sem.at[t]) for t, ref in enumerate((targets, sources))
-    ]
-    for read in reads:
-        read.start()
-
     barrier = pltpu.get_barrier_semaphore()
     for d in range(1, nc):
         pl.semaphore_signal(barrier, inc=1, device_id=(c, line(d) * q + y), device_id_type=MESH)
@@ -74,9 +68,8 @@
     def own_rows(t, block, owner=me):
         return alls.at[t, pl.ds(pl.multiple_of(owner * rows + block * per, per), per)]
 
-    def into_slots(t, ordering):
-        reads[t].wait()
-        slots = jnp.dot(selector(ordering), given[t], preferred_element_type=jnp.float32)
+    def into_slots(t, ordering, matrix):
+        slots = jnp.dot(selector(ordering), matrix[...], preferred_element_type=jnp.float32)
         sent[t] = slots.astype(jnp.bfloat16)
         own_rows(t, 0)[...] = sent[t, pl.ds(pl.multiple_of(k * per, per), per)]
 
@@ -90,16 +83,11 @@
             device_id_type=MESH,
         )
 
-    into_slots(0, target_order)
+    into_slots(0, target_order, targets)
     pl.semaphore_wait(barrier, nc - 1 + nr - 1)
-    line_copies = []
-    for t in range(2):
-        if t == 1:
-            into_slots(1, source_order)
-        for d in range(1, nc):
-            copy = line_copy(t, d)
-            copy.start()
-            line_copies.append(copy)
+    for d in range(1, nc):
+        line_copy(0, d).start()
+    into_slots(1, source_order, sources)
 
     counts = [0, 0]
 
@@ -150,6 +138,8 @@
                         send_sem=own_send.at[t, nc - j], recv_sem=own_recv.at[t, nc - j],
                         device_id=(c, line(j) * q + y), device_id_type=MESH,
                     ).wait_recv()
+                    if t == 0:
+                        line_copy(1, nc - j).start()
             first, second = axes(i)
             for step in range(1, first):
                 forward(t, i, here, at(along(i, step, 0)))
@@ -279,13 +269,14 @@
     gather_own(0)
     gather_first(0)
     gather_second(0)
+    gather_own(1)
     square_panels(0, core)
+    build(1, core)
     for dx in range(nx):
         for dy in range(q):
             gather_sibling(0, at((dx, dy), sibling_core))
     square_panels(0, sibling_core)
-    gather_own(1)
-    build(1, core)
+    gather_first(1)
     build(1, sibling_core)
 
     potentials[1] = jnp.zeros_like(potentials[1])
@@ -302,11 +293,10 @@
 
         @pl.when(repeat == 0)
         def _():
-            gather_first(1)
+            gather_second(1)
 
         @pl.when(repeat == 1)
         def _():
-            gather_second(1)
             square_panels(1, core)
             build(0, core)
 
@@ -385,9 +375,9 @@
 
     lax.fori_loop(0, 2, both_maps, 0)
 
-    for copy in line_copies:
-        copy.wait_send()
     for t in range(2):
+        for d in range(1, nc):
+            line_copy(t, d).wait_send()
         for number in range(counts[t]):
             pltpu.make_async_remote_copy(
                 src_ref=chunk_rows(t, 0, me), dst_ref=chunk_rows(t, 0, me),
@@ -405,14 +395,8 @@
             selector(ordering), back[t], (((0,), (0,)), ((), ())), preferred_element_type=jnp.float32
         ).astype(jnp.bfloat16)
 
-    writes = []
-    for t, (ordering, out) in enumerate(((target_order, target_out), (source_order, source_out))):
-        given[t] = out_of_slots(t, ordering)
-        write = pltpu.make_async_copy(given.at[t], out, in_sem.at[t])
-        write.start()
-        writes.append(write)
-    for write in writes:
-        write.wait()
+    target_out[...] = out_of_slots(0, target_order)
+    source_out[...] = out_of_slots(1, source_order)
 
 
 def solution(mesh):
@@ -434,10 +418,9 @@
         return pl.pallas_call(
             functools.partial(kernel, nc, nr),
             out_shape=(out, out),
-            in_specs=[pl.BlockSpec(memory_space=pl.ANY)] * 2 + [vmem] * 2,
-            out_specs=(pl.BlockSpec(memory_space=pl.ANY),) * 2,
+            in_specs=[vmem] * 4,
+            out_specs=(vmem, vmem),
             scratch_shapes=[
-                pltpu.VMEM((2, rows, width), jnp.bfloat16),
                 pltpu.VMEM((2, columns, width), jnp.bfloat16),
                 pltpu.VMEM((2, rows, width), jnp.bfloat16),
                 pltpu.VMEM((2, rows, width), jnp.bfloat16),
@@ -449,12 +432,12 @@
                 pltpu.VMEM((blocks, LANES), jnp.float32),
                 pltpu.VMEM((blocks, LANES), jnp.float32),
                 pltpu.VMEM((ITERS, nr, blocks + 8, LANES), jnp.float32),
-                dma((2,)), dma((2, nc)), dma((2, nc)), dma((2, nc)), dma((2, nc)),
+                dma((2, nc)), dma((2, nc)), dma((2, nc)), dma((2, nc)),
                 dma((2, copies)), dma((2, chunks, nr)),
                 dma((ITERS, nr)), dma((ITERS, nr)),
             ],
             compiler_params=pltpu.CompilerParams(
-                collective_id=0, has_side_effects=True, vmem_limit_bytes=63 * 1024 * 1024
+                collective_id=0, has_side_effects=True, vmem_limit_bytes=48 * 1024 * 1024
             ),
         )(sources, targets, source_order.reshape(1, rows), target_order.reshape(1, rows))
 

time: 62.3 us -> 64.9 us (1.042)
  local copies, waits for them, and re-layouts: 2.42 us -> 3.99 us
  Pallas kernels: 59.1 us -> 60.1 us
    unnamed x4 -> x10, local copies, waits for them, and re-layouts: 2.42 us -> 3.99 us
    pallas_call x1, Pallas kernels: 59.1 us -> 60.1 us  [shards(): pl.pallas_call(functools.partial(kernel, nc, nr), out_shape=(out, out), i...]
where the time goes in v4:
time: 64.9 us; the launch traced here: 64.7 us
  Pallas kernels  60.1 us (93%)
  local copies, waits for them, and re-layouts  3.99 us (6%)
  between operations  0.66 us (1%)
    pallas_call x1, Pallas kernels, shards(): pl.pallas_call(functools.partial(kernel, nc, nr), out_shape=(out, out), i...  60.1 us
    unnamed x10, local copies, waits for them, and re-layouts  3.99 us

profile of v4, /device:TPU:0, one launch (start us, length us, event | category | flops | bytes accessed | tf_op | source)
XLA Modules:
  0.0 64.7 jit_solution(11343649913165929985)
XLA Ops:
  0.6 0.0 copy-start.3
  0.6 0.0 copy-start.2
  0.7 0.7 %copy-done.3 = s32[256]{0:T(256)S(1)} copy-done((s32[256]{0:T(256)S(1)}, s32[256]{0:T(256)}, u32[]{:S(2)}) %copy-start.3) | copy-done | bytes 1048
  1.3 0.0 copy-done.2
  1.3 0.0 copy-start
  1.3 0.9 %copy-done = bf16[256,512]{1,0:T(8,128)(2,1)S(1)} copy-done((bf16[256,512]{1,0:T(8,128)(2,1)S(1)}, bf16[256,512]{1,0:T(8,128)(2,1)}, u32[]{:S(2)}) %copy-start) | copy-done | bytes 262168
  2.3 0.0 copy-start.1
  2.3 0.9 %copy-done.1 = bf16[256,512]{1,0:T(8,128)(2,1)S(1)} copy-done((bf16[256,512]{1,0:T(8,128)(2,1)S(1)}, bf16[256,512]{1,0:T(8,128)(2,1)}, u32[]{:S(2)}) %copy-start.1) | copy-done | bytes 262168
  3.2 60.1 %shard_map.59 = (bf16[256,512]{1,0:T(8,128)(2,1)S(1)}, bf16[256,512]{1,0:T(8,128)(2,1)S(1)}) custom-call(bf16[256,512]{1,0:T(8,128)(2,1)S(1)} %copy-done, bf16[256,512]{1,0:T(8,128)(2,1)S(1)} %copy-done.1, s32[1,256]{1,0:T(1,128)S(1)} %bitcast.2, s32[1,256]{1,0:T(1,128)S(1)} %bitcast.3), custom_call_target="tpu_custom_call" | custom-call | tf_op jit(solution)/shard_map/pallas_call | solution.py:418
  63.3 0.7 %copy.8 = bf16[256,512]{1,0:T(8,128)(2,1)} copy(bf16[256,512]{1,0:T(8,128)(2,1)S(1)} %get-tuple-element.4) | data formatting | bytes 524288
  64.0 0.7 %copy.9 = bf16[256,512]{1,0:T(8,128)(2,1)} copy(bf16[256,512]{1,0:T(8,128)(2,1)S(1)} %get-tuple-element.5) | data formatting | bytes 524288
Async XLA Ops:
  0.6 0.7 %copy-start.3 = (s32[256]{0:T(256)S(1)}, s32[256]{0:T(256)}, u32[]{:S(2)}) copy-start(s32[256]{0:T(256)} %param.7) | copy-start | bytes 3076
  0.6 0.7 %copy-start.2 = (s32[256]{0:T(256)S(1)}, s32[256]{0:T(256)}, u32[]{:S(2)}) copy-start(s32[256]{0:T(256)} %param.6) | copy-start | bytes 3076
  1.3 0.9 %copy-start = (bf16[256,512]{1,0:T(8,128)(2,1)S(1)}, bf16[256,512]{1,0:T(8,128)(2,1)}, u32[]{:S(2)}) copy-start(bf16[256,512]{1,0:T(8,128)(2,1)} %sources.1) | copy-start | bytes 786436
  2.3 0.9 %copy-start.1 = (bf16[256,512]{1,0:T(8,128)(2,1)S(1)}, bf16[256,512]{1,0:T(8,128)(2,1)}, u32[]{:S(2)}) copy-start(bf16[256,512]{1,0:T(8,128)(2,1)} %targets.1) | copy-start | bytes 786436

commit v5 on v1

--- a/solution.py
+++ b/solution.py
@@ -300,11 +300,16 @@
             gather_first(1)
         if repeat == 1:
             gather_second(1)
+            panel = build(cost_t, all_t, all_s, lambda index: member(
+                index // q, core, lax.rem(index, q)))
+            lax.fori_loop(0, nx * q, panel, 0)
         if last:
             for dx in range(nx):
                 for dy in range(q):
                     gather_sibling(1, at((dx, dy), sibling_core))
-            lax.fori_loop(0, nr, build(cost_t, all_t, all_s, lambda index: index), 0)
+            panel = build(cost_t, all_t, all_s, lambda index: member(
+                index // q, sibling_core, lax.rem(index, q)))
+            lax.fori_loop(0, nx * q, panel, 0)
         for number, other in enumerate(others):
             owner = member(*other)
             pltpu.make_async_remote_copy(
@@ -338,8 +343,6 @@
         own = pl.ds(pl.multiple_of(k * per, per), per)
         back[t, own] = maps[t, own]
 
-    maps[1] = mapped(cost_s, potential, row_lse(cost_s, potential), all_t)
-    send_back(1)
     for m in range(nr):
         source_row[m * own_blocks : (m + 1) * own_blocks, :] = parts[
             ITERS - 1, m, blocks : blocks + own_blocks, :
@@ -347,6 +350,8 @@
     own_norm = [to_column(sums[pl.ds(me * own_blocks + b, 1), :]) for b in range(own_blocks)]
     maps[0] = mapped(cost_t, source_row, own_norm, all_s)
     send_back(0)
+    maps[1] = mapped(cost_s, potential, row_lse(cost_s, potential), all_t)
+    send_back(1)
 
     for copy in line_copies + sent_copies + part_copies:
         copy.wait_send()
@@ -358,8 +363,8 @@
             selector(ordering), back[t], (((0,), (0,)), ((), ())), preferred_element_type=jnp.float32
         ).astype(jnp.bfloat16)
 
+    target_out[...] = out_of_slots(0, target_order)
     source_out[...] = out_of_slots(1, source_order)
-    target_out[...] = out_of_slots(0, target_order)
 
 
 def solution(mesh):

time: 59.1 us -> 58.8 us (level)
  no operation moved by 1% of the time
where the time goes in v5:
time: 58.8 us; the launch traced here: 58.6 us
  Pallas kernels  53.9 us (92%)
  local copies, waits for them, and re-layouts  3.99 us (7%)
  between operations  0.66 us (1%)
    pallas_call x1, Pallas kernels, shards(): pl.pallas_call(functools.partial(kernel, nc, nr), out_shape=(out, out), i...  53.9 us
    unnamed x10, local copies, waits for them, and re-layouts  3.99 us

profile of v5, /device:TPU:0, one launch (start us, length us, event | category | flops | bytes accessed | tf_op | source)
XLA Modules:
  0.0 58.6 jit_solution(3424791325581462252)
XLA Ops:
  0.6 0.0 copy-start.3
  0.6 0.0 copy-start.2
  0.7 0.7 %copy-done.3 = s32[256]{0:T(256)S(1)} copy-done((s32[256]{0:T(256)S(1)}, s32[256]{0:T(256)}, u32[]{:S(2)}) %copy-start.3) | copy-done | bytes 1048
  1.3 0.0 copy-done.2
  1.3 0.0 copy-start
  1.3 0.9 %copy-done = bf16[256,512]{1,0:T(8,128)(2,1)S(1)} copy-done((bf16[256,512]{1,0:T(8,128)(2,1)S(1)}, bf16[256,512]{1,0:T(8,128)(2,1)}, u32[]{:S(2)}) %copy-start) | copy-done | bytes 262168
  2.3 0.0 copy-start.1
  2.3 0.9 %copy-done.1 = bf16[256,512]{1,0:T(8,128)(2,1)S(1)} copy-done((bf16[256,512]{1,0:T(8,128)(2,1)S(1)}, bf16[256,512]{1,0:T(8,128)(2,1)}, u32[]{:S(2)}) %copy-start.1) | copy-done | bytes 262168
  3.2 53.9 %shard_map.59 = (bf16[256,512]{1,0:T(8,128)(2,1)S(1)}, bf16[256,512]{1,0:T(8,128)(2,1)S(1)}) custom-call(bf16[256,512]{1,0:T(8,128)(2,1)S(1)} %copy-done, bf16[256,512]{1,0:T(8,128)(2,1)S(1)} %copy-done.1, s32[1,256]{1,0:T(1,128)S(1)} %bitcast.2, s32[1,256]{1,0:T(1,128)S(1)} %bitcast.3), custom_call_target="tpu_custom_call" | custom-call | tf_op jit(solution)/shard_map/pallas_call | solution.py:386
  57.1 0.7 %copy.8 = bf16[256,512]{1,0:T(8,128)(2,1)} copy(bf16[256,512]{1,0:T(8,128)(2,1)S(1)} %get-tuple-element.4) | data formatting | bytes 524288
  57.9 0.7 %copy.9 = bf16[256,512]{1,0:T(8,128)(2,1)} copy(bf16[256,512]{1,0:T(8,128)(2,1)S(1)} %get-tuple-element.5) | data formatting | bytes 524288
Async XLA Ops:
  0.6 0.7 %copy-start.3 = (s32[256]{0:T(256)S(1)}, s32[256]{0:T(256)}, u32[]{:S(2)}) copy-start(s32[256]{0:T(256)} %param.7) | copy-start | bytes 3076
  0.6 0.7 %copy-start.2 = (s32[256]{0:T(256)S(1)}, s32[256]{0:T(256)}, u32[]{:S(2)}) copy-start(s32[256]{0:T(256)} %param.6) | copy-start | bytes 3076
  1.3 0.9 %copy-start = (bf16[256,512]{1,0:T(8,128)(2,1)S(1)}, bf16[256,512]{1,0:T(8,128)(2,1)}, u32[]{:S(2)}) copy-start(bf16[256,512]{1,0:T(8,128)(2,1)} %sources.1) | copy-start | bytes 786436
  2.3 0.9 %copy-start.1 = (bf16[256,512]{1,0:T(8,128)(2,1)S(1)}, bf16[256,512]{1,0:T(8,128)(2,1)}, u32[]{:S(2)}) copy-start(bf16[256,512]{1,0:T(8,128)(2,1)} %targets.1) | copy-start | bytes 786436

commit v6 on v1

--- a/solution.py
+++ b/solution.py
@@ -301,10 +301,9 @@
         if repeat == 1:
             gather_second(1)
         if last:
-            for dx in range(nx):
-                for dy in range(q):
-                    gather_sibling(1, at((dx, dy), sibling_core))
-            lax.fori_loop(0, nr, build(cost_t, all_t, all_s, lambda index: index), 0)
+            panel = build(cost_t, all_t, all_s, lambda index: member(
+                index // q, core, lax.rem(index, q)))
+            lax.fori_loop(0, nx * q, panel, 0)
         for number, other in enumerate(others):
             owner = member(*other)
             pltpu.make_async_remote_copy(
@@ -340,6 +339,12 @@
 
     maps[1] = mapped(cost_s, potential, row_lse(cost_s, potential), all_t)
     send_back(1)
+    for dx in range(nx):
+        for dy in range(q):
+            gather_sibling(1, at((dx, dy), sibling_core))
+    panel = build(cost_t, all_t, all_s, lambda index: member(
+        index // q, sibling_core, lax.rem(index, q)))
+    lax.fori_loop(0, nx * q, panel, 0)
     for m in range(nr):
         source_row[m * own_blocks : (m + 1) * own_blocks, :] = parts[
             ITERS - 1, m, blocks : blocks + own_blocks, :

time: 59.1 us -> 59.1 us (level)
  no operation moved by 1% of the time
where the time goes in v6:
time: 59.1 us; the launch traced here: 58.9 us
  Pallas kernels  54.3 us (92%)
  local copies, waits for them, and re-layouts  3.99 us (7%)
  between operations  0.66 us (1%)
    pallas_call x1, Pallas kernels, shards(): pl.pallas_call(functools.partial(kernel, nc, nr), out_shape=(out, out), i...  54.3 us
    unnamed x10, local copies, waits for them, and re-layouts  3.99 us

profile of v6, /device:TPU:0, one launch (start us, length us, event | category | flops | bytes accessed | tf_op | source)
XLA Modules:
  0.0 58.9 jit_solution(74712818841327227)
XLA Ops:
  0.6 0.0 copy-start.3
  0.6 0.0 copy-start.2
  0.7 0.7 %copy-done.3 = s32[256]{0:T(256)S(1)} copy-done((s32[256]{0:T(256)S(1)}, s32[256]{0:T(256)}, u32[]{:S(2)}) %copy-start.3) | copy-done | bytes 1048
  1.3 0.0 copy-done.2
  1.3 0.0 copy-start
  1.3 0.9 %copy-done = bf16[256,512]{1,0:T(8,128)(2,1)S(1)} copy-done((bf16[256,512]{1,0:T(8,128)(2,1)S(1)}, bf16[256,512]{1,0:T(8,128)(2,1)}, u32[]{:S(2)}) %copy-start) | copy-done | bytes 262168
  2.3 0.0 copy-start.1
  2.3 0.9 %copy-done.1 = bf16[256,512]{1,0:T(8,128)(2,1)S(1)} copy-done((bf16[256,512]{1,0:T(8,128)(2,1)S(1)}, bf16[256,512]{1,0:T(8,128)(2,1)}, u32[]{:S(2)}) %copy-start.1) | copy-done | bytes 262168
  3.2 54.3 %shard_map.59 = (bf16[256,512]{1,0:T(8,128)(2,1)S(1)}, bf16[256,512]{1,0:T(8,128)(2,1)S(1)}) custom-call(bf16[256,512]{1,0:T(8,128)(2,1)S(1)} %copy-done, bf16[256,512]{1,0:T(8,128)(2,1)S(1)} %copy-done.1, s32[1,256]{1,0:T(1,128)S(1)} %bitcast.2, s32[1,256]{1,0:T(1,128)S(1)} %bitcast.3), custom_call_target="tpu_custom_call" | custom-call | tf_op jit(solution)/shard_map/pallas_call | solution.py:386
  57.5 0.7 %copy.8 = bf16[256,512]{1,0:T(8,128)(2,1)} copy(bf16[256,512]{1,0:T(8,128)(2,1)S(1)} %get-tuple-element.4) | data formatting | bytes 524288
  58.2 0.7 %copy.9 = bf16[256,512]{1,0:T(8,128)(2,1)} copy(bf16[256,512]{1,0:T(8,128)(2,1)S(1)} %get-tuple-element.5) | data formatting | bytes 524288
Async XLA Ops:
  0.6 0.7 %copy-start.3 = (s32[256]{0:T(256)S(1)}, s32[256]{0:T(256)}, u32[]{:S(2)}) copy-start(s32[256]{0:T(256)} %param.7) | copy-start | bytes 3076
  0.6 0.7 %copy-start.2 = (s32[256]{0:T(256)S(1)}, s32[256]{0:T(256)}, u32[]{:S(2)}) copy-start(s32[256]{0:T(256)} %param.6) | copy-start | bytes 3076
  1.3 0.9 %copy-start = (bf16[256,512]{1,0:T(8,128)(2,1)S(1)}, bf16[256,512]{1,0:T(8,128)(2,1)}, u32[]{:S(2)}) copy-start(bf16[256,512]{1,0:T(8,128)(2,1)} %sources.1) | copy-start | bytes 786436
  2.3 0.9 %copy-start.1 = (bf16[256,512]{1,0:T(8,128)(2,1)S(1)}, bf16[256,512]{1,0:T(8,128)(2,1)}, u32[]{:S(2)}) copy-start(bf16[256,512]{1,0:T(8,128)(2,1)} %targets.1) | copy-start | bytes 786436
